TPU v7x, 512 devices: a whole 4x8x8 slice. The times are simulated.
512 devices in a mesh: expert: 64 (over x, y, core), tensor: 8 (over z).
Axes of the slice: x: 4, y: 8, z: 8, core: 2. Of those that a mesh axis runs over, the one named last changes fastest.
Arguments:
- tokens: bfloat16 [8192, 5120], P('expert', 'tensor'), may hold values from -6 to 6
- out_grad: bfloat16 [8192, 5120], P('expert', 'tensor'), may hold values from -6 to 6
- expert_ids: int32 [8192, 2], P('expert'), may hold values from 0 to 15, all different within a row; in each aligned block of 128 rows (0 to 127, 128 to 255, ...) at most 17 rows name the same one
- gate_probs: float32 [8192, 2], P('expert'), may hold values from 0.2 to 1
- w_gate: bfloat16 [5120, 38912], P('tensor', 'expert'), may hold values from -0.078125 to 0.078125
- w_up: bfloat16 [5120, 38912], P('tensor', 'expert'), may hold values from -0.078125 to 0.078125
- w_down: bfloat16 [38912, 5120], P('expert', 'tensor'), may hold values from -0.125 to 0.125
Outputs:
- grad_tokens: bfloat16 [8192, 5120], P('expert', 'tensor')
- grad_gate: bfloat16 [5120, 38912], P('tensor', 'expert')
- grad_up: bfloat16 [5120, 38912], P('tensor', 'expert')
- grad_down: bfloat16 [38912, 5120], P('expert', 'tensor')
Inputs may be any that keep to these rules, and one draw needn't show every extreme that they name: `expert_ids`: each row names two different experts. Among the tokens of one index of the expert axis (aligned blocks of 128 rows) no expert is named more than 17 times, and in every draw some expert is named exactly 17 times in some block.
All inputs are finite; a program needn't handle non-finite values.
Results may differ from a plain program's by a relative error of at most 0.029.
Values may be sent and summed in bfloat16 or wider, within the bound.
No kernel may reach another device: no remote copies, remote signals or barrier semaphores. Data moves between devices by JAX's collectives and lax.ppermute only.
A program may use at most 64 MiB of HBM per device.

v0:
```python
import jax
import jax.numpy as jnp
from jax import lax
from jax.sharding import PartitionSpec as P

MEMBERS = 4


def activations(gate, up, grad_hidden):
    sigma = jax.nn.sigmoid(gate)
    silu = gate * sigma
    hidden = (silu * up).astype(jnp.bfloat16)
    grad_act_gate = (grad_hidden * up * sigma * (1.0 + gate * (1.0 - sigma))).astype(jnp.bfloat16)
    grad_act_up = (grad_hidden * silu).astype(jnp.bfloat16)
    return (hidden, grad_act_gate, grad_act_up)


def on_device(tokens, out_grad, expert_ids, gate_probs, w_gate, w_up, w_down):
    token_row_block = tokens.shape[0]
    columns = tokens.shape[1]
    devices = lax.axis_size("expert")
    groups = devices // MEMBERS
    capacity = min(
        token_row_block, 2 * token_row_block // groups + max(1, token_row_block // (8 * groups))
    )
    flat_ids = expert_ids.reshape(-1)
    one_hot = (flat_ids[:, None] == jnp.arange(groups, dtype=jnp.int32)[None, :]).astype(jnp.int32)
    slot_index = jnp.sum((jnp.cumsum(one_hot, axis=0) - 1) * one_hot, axis=1)
    target = flat_ids * capacity + slot_index
    placing = (jnp.arange(groups * capacity, dtype=jnp.int32)[:, None] == target[None, :]).astype(
        jnp.bfloat16
    )
    rows_x = jnp.repeat(tokens, 2, axis=0)
    scaled = (
        jnp.repeat(out_grad, 2, axis=0).astype(jnp.float32) * gate_probs.reshape(-1)[:, None]
    ).astype(jnp.bfloat16)

    def fan_out(rows):
        packed = jnp.dot(placing, rows, preferred_element_type=jnp.float32).astype(jnp.bfloat16)
        packed = packed.reshape(groups, 1, capacity, columns)
        return jnp.broadcast_to(packed, (groups, MEMBERS, capacity, columns)).reshape(
            devices, capacity, columns
        )

    send_x = fan_out(rows_x)
    send_grad = fan_out(scaled)
    received_input, recv_grad = (
        lax.all_to_all(send_x, "expert", split_axis=0, concat_axis=0, tiled=True),
        lax.all_to_all(send_grad, "expert", split_axis=0, concat_axis=0, tiled=True),
    )
    local_x = received_input.reshape(devices * capacity, columns)
    local_grad = recv_grad.reshape(devices * capacity, columns)
    gate_part = jnp.dot(local_x, w_gate, preferred_element_type=jnp.float32)
    up_part = jnp.dot(local_x, w_up, preferred_element_type=jnp.float32)
    hidden_part = jnp.dot(local_grad, w_down.T, preferred_element_type=jnp.float32)
    gate, up, grad_hidden = (
        lax.psum(gate_part.astype(jnp.bfloat16), "tensor").astype(jnp.float32),
        lax.psum(up_part.astype(jnp.bfloat16), "tensor").astype(jnp.float32),
        lax.psum(hidden_part.astype(jnp.bfloat16), "tensor").astype(jnp.float32),
    )
    hidden, grad_act_gate, grad_act_up = activations(gate, up, grad_hidden)
    grad_down = jnp.dot(hidden.T, local_grad, preferred_element_type=jnp.float32).astype(
        jnp.bfloat16
    )
    grad_gate = jnp.dot(local_x.T, grad_act_gate, preferred_element_type=jnp.float32).astype(
        jnp.bfloat16
    )
    grad_up = jnp.dot(local_x.T, grad_act_up, preferred_element_type=jnp.float32).astype(
        jnp.bfloat16
    )
    partial_rows = jnp.dot(grad_act_gate, w_gate.T, preferred_element_type=jnp.float32)
    partial_rows = partial_rows + jnp.dot(grad_act_up, w_up.T, preferred_element_type=jnp.float32)
    partial_rows = partial_rows.astype(jnp.bfloat16)
    returned = lax.all_to_all(
        partial_rows.reshape(devices, capacity, columns),
        "expert",
        split_axis=0,
        concat_axis=0,
        tiled=True,
    )
    summed = (
        returned.astype(jnp.float32)
        .reshape(groups, MEMBERS, capacity, columns)
        .sum(axis=1)
        .reshape(groups * capacity, columns)
    )
    token_parts = jnp.dot(placing.astype(jnp.float32).T, summed, precision=lax.Precision.HIGHEST)
    grad_tokens = token_parts.reshape(token_row_block, 2, columns).sum(axis=1).astype(jnp.bfloat16)
    return (grad_tokens, grad_gate, grad_up, grad_down)


def solution(mesh):
    placed = (
        P("expert", "tensor"),
        P("expert", "tensor"),
        P("expert", None),
        P("expert", None),
        P("tensor", "expert"),
        P("tensor", "expert"),
        P("expert", "tensor"),
    )
    return jax.shard_map(
        on_device,
        mesh=mesh,
        in_specs=placed,
        out_specs=(
            P("expert", "tensor"),
            P("tensor", "expert"),
            P("tensor", "expert"),
            P("expert", "tensor"),
        ),
        check_vma=False,
    )
```

profile of v0, /device:TPU:1, one launch (start us, length us, event | category | flops | bytes accessed | tf_op | source)
XLA Modules:
  0.0 327.9 jit_solution(3972749489903727645)
XLA Ops:
  7.2 0.9 copy.11
  8.3 0.6 reduce-window.6
  9.2 1.1 broadcast_in_dim.26
  10.9 1.5 broadcast_in_dim.28
  12.4 11.8 %all-to-all-start.1 = ((bf16[64,17,640]{2,1,0:T(8,128)(2,1)}), bf16[64,17,640]{2,1,0:T(8,128)(2,1)S(1)}, u32[]{:S(2)}, u32[]{:S(2)}) async-start(bf16[64,17,640]{2,1,0:T(8,128)(2,1)} %bitcast.35), calls=%async_computation.1 | async-start | bytes 3932160 | tf_op jit(solution)/shard_map/all_to_all | solution.py:48
  24.1 1.0 broadcast_in_dim.23
  25.2 1.5 convert_element_type.68
  27.0 1.1 convolution_convert_fusion.7
  28.0 1.1 broadcast_in_dim.24
  29.2 43.2 %all-to-all-done.1 = bf16[64,17,640]{2,1,0:T(8,128)(2,1)S(1)} async-done(((bf16[64,17,640]{2,1,0:T(8,128)(2,1)}), bf16[64,17,640]{2,1,0:T(8,128)(2,1)S(1)}, u32[]{:S(2)}, u32[]{:S(2)}) %all-to-all-start.1) | async-done | bytes 1392672 | tf_op jit(solution)/shard_map/all_to_all | solution.py:48
  72.3 1.5 broadcast_in_dim.25
  73.8 6.2 %all-to-all-start = ((bf16[64,17,640]{2,1,0:T(8,128)(2,1)}), bf16[64,17,640]{2,1,0:T(8,128)(2,1)}, u32[]{:S(2)}, u32[]{:S(2)}) async-start(bf16[64,17,640]{2,1,0:T(8,128)(2,1)} %bitcast.36), calls=%async_computation | async-start | bytes 3932160 | tf_op jit(solution)/shard_map/all_to_all | solution.py:49
  80.3 1.4 reshape.104
  81.7 4.1 %convolution_convert_fusion = bf16[1088,608]{1,0:T(8,128)(2,1)} fusion(bf16[1088,640]{1,0:T(8,128)(2,1)} %reshape.104, bf16[640,608]{0,1:T(8,128)(2,1)S(1)} %copy-done), kind=kOutput, calls=%fused_computation.9 | convolution fusion | flops 847386624 | bytes 3493888 | tf_op jit(solution)/shard_map/dot_general | solution.py:53
  85.8 2.5 convolution_convert_fusion.1
  88.3 39.9 %all-to-all-done = bf16[64,17,640]{2,1,0:T(8,128)(2,1)} async-done(((bf16[64,17,640]{2,1,0:T(8,128)(2,1)}), bf16[64,17,640]{2,1,0:T(8,128)(2,1)}, u32[]{:S(2)}, u32[]{:S(2)}) %all-to-all-start) | async-done | bytes 1392672 | tf_op jit(solution)/shard_map/all_to_all | solution.py:49
  128.2 2.5 reshape.101
  130.7 2.5 convolution_convert_fusion.2
  133.3 115.9 %all-reduce.3.cloned.1.call-done = (bf16[1088,608]{1,0:T(8,128)(2,1)}, bf16[1088,608]{1,0:T(8,128)(2,1)}, bf16[1088,608]{1,0:T(8,128)(2,1)}) async-done(((bf16[1088,608]{1,0:T(8,128)(2,1)}, bf16[1088,608]{1,0:T(8,128)(2,1)}, bf16[1088,608]{1,0:T(8,128)(2,1)}), (bf16[1088,608]{1,0:T(8,128)(2,1)}, bf16[1088,608]{1,0:T(8,128)(2,1)}, bf16[1088,608]{1,0:T(8,128)(2,1)})) %all-reduce.3.cloned.1.call-update) | async-done | bytes 3969040 | tf_op jit(solution)/shard_map/psum | solution.py:58
  249.2 3.4 %fusion.4 = bf16[1088,608]{1,0:T(8,128)(2,1)S(1)} fusion(bf16[1088,608]{1,0:T(8,128)(2,1)} %get-tuple-element.4, bf16[1088,608]{1,0:T(8,128)(2,1)} %get-tuple-element.5, bf16[1088,608]{1,0:T(8,128)(2,1)} %get-tuple-element.6), kind=kLoop, calls=%fused_computation.15 | loop fusion | flops 8599552 | bytes 5292032 | tf_op jit(solution)/shard_map/convert_element_type | solution.py:13
  252.7 1.4 fusion.21
  254.1 0.4 copy-done.6
  255.1 1.7 fusion
  256.8 1.6 reshape.105
  258.4 10.4 %all-to-all-start.2 = ((bf16[64,17,640]{2,1,0:T(8,128)(2,1)}), bf16[64,17,640]{2,1,0:T(8,128)(2,1)S(1)}, u32[]{:S(2)}, u32[]{:S(2)}) async-start(bf16[64,17,640]{2,1,0:T(8,128)(2,1)} %reshape.105), calls=%async_computation.2 | async-start | bytes 3932160 | tf_op jit(solution)/shard_map/all_to_all | solution.py:74
  269.1 4.2 %convolution_convert_fusion.5 = bf16[640,608]{0,1:T(8,128)(2,1)} fusion(bf16[1088,640]{1,0:T(8,128)(2,1)} %reshape.104, bf16[1088,608]{1,0:T(8,128)(2,1)} %copy-done.10), kind=kOutput, calls=%fused_computation.23 | convolution fusion | flops 847114240 | bytes 3493888 | tf_op jit(solution)/shard_map/dot_general | solution.py:65
  273.3 2.5 convolution_convert_fusion.4
  275.8 2.5 convolution_convert_fusion.3
  278.3 38.7 %all-to-all-done.2 = bf16[64,17,640]{2,1,0:T(8,128)(2,1)S(1)} async-done(((bf16[64,17,640]{2,1,0:T(8,128)(2,1)}), bf16[64,17,640]{2,1,0:T(8,128)(2,1)S(1)}, u32[]{:S(2)}, u32[]{:S(2)}) %all-to-all-start.2) | async-done | bytes 1392672 | tf_op jit(solution)/shard_map/all_to_all | solution.py:74
  317.0 1.2 convert_reduce_fusion
  318.3 1.3 reshape.111
  319.6 1.5 convolution_reduce_fusion
  (48 shorter events, 2.6 us)
Async XLA Ops:
  7.2 74.5 %copy-start = (bf16[640,608]{0,1:T(8,128)(2,1)S(1)}, bf16[640,608]{0,1:T(8,128)(2,1)}, u32[]{:S(2)}) copy-start(bf16[640,608]{0,1:T(8,128)(2,1)} %param.11) | copy-start | bytes 2334724
  12.4 11.8 %copy-start.11 = (bf16[128,640]{1,0:T(8,128)(2,1)S(1)}, bf16[128,640]{1,0:T(8,128)(2,1)}, u32[]{:S(2)}) copy-start(bf16[128,640]{1,0:T(8,128)(2,1)} %param.8) | copy-start | bytes 491524
  12.4 60.0 %all-to-all-start.1 = ((bf16[64,17,640]{2,1,0:T(8,128)(2,1)}), bf16[64,17,640]{2,1,0:T(8,128)(2,1)S(1)}, u32[]{:S(2)}, u32[]{:S(2)}) async-start(bf16[64,17,640]{2,1,0:T(8,128)(2,1)} %bitcast.35), calls=%async_computation.1 | async-start | bytes 3932160 | tf_op jit(solution)/shard_map/all_to_all | solution.py:48
  24.1 2.6 copy-start.12
  73.8 54.4 %all-to-all-start = ((bf16[64,17,640]{2,1,0:T(8,128)(2,1)}), bf16[64,17,640]{2,1,0:T(8,128)(2,1)}, u32[]{:S(2)}, u32[]{:S(2)}) async-start(bf16[64,17,640]{2,1,0:T(8,128)(2,1)} %bitcast.36), calls=%async_computation | async-start | bytes 3932160 | tf_op jit(solution)/shard_map/all_to_all | solution.py:49
  80.0 169.2 %all-reduce.3.cloned.1.call-start = ((), (), s32[]{:S(2)}) async-start(), calls=%async_computation.3 | async-start | bytes 8355840 | tf_op jit(solution)/shard_map/psum | solution.py:58
  81.7 4.1 %copy-start.1 = (bf16[1088,640]{1,0:T(8,128)(2,1)S(1)}, bf16[1088,640]{1,0:T(8,128)(2,1)}, u32[]{:S(2)}) copy-start(bf16[1088,640]{1,0:T(8,128)(2,1)} %reshape.104) | copy-start | bytes 4177924
  81.7 4.1 %copy-start.14 = (bf16[640,608]{0,1:T(8,128)(2,1)S(1)}, bf16[640,608]{0,1:T(8,128)(2,1)}, u32[]{:S(2)}) copy-start(bf16[640,608]{0,1:T(8,128)(2,1)} %param.12) | copy-start | bytes 2334724
  88.3 42.4 %copy-start.13 = (bf16[608,640]{1,0:T(8,128)(2,1)S(1)}, bf16[608,640]{1,0:T(8,128)(2,1)}, u32[]{:S(2)}) copy-start(bf16[608,640]{1,0:T(8,128)(2,1)} %param.13) | copy-start | bytes 2334724
  130.7 2.5 copy-start.3
  252.6 1.4 copy-start.10
  252.7 1.9 copy-start.6
  252.7 2.3 copy-start.8
  252.7 2.5 copy-start.15
  258.4 58.6 %all-to-all-start.2 = ((bf16[64,17,640]{2,1,0:T(8,128)(2,1)}), bf16[64,17,640]{2,1,0:T(8,128)(2,1)S(1)}, u32[]{:S(2)}, u32[]{:S(2)}) async-start(bf16[64,17,640]{2,1,0:T(8,128)(2,1)} %reshape.105), calls=%async_computation.2 | async-start | bytes 3932160 | tf_op jit(solution)/shard_map/all_to_all | solution.py:74
  269.1 4.2 %copy-start.2 = (bf16[1088,640]{1,0:T(8,128)(2,1)S(1)}, bf16[1088,640]{1,0:T(8,128)(2,1)}, u32[]{:S(2)}) copy-start(bf16[1088,640]{1,0:T(8,128)(2,1)} %reshape.104) | copy-start | bytes 4177924
  269.1 4.2 %copy-start.7 = (bf16[1088,608]{1,0:T(8,128)(2,1)S(1)}, bf16[1088,608]{1,0:T(8,128)(2,1)}, u32[]{:S(2)}) copy-start(bf16[1088,608]{1,0:T(8,128)(2,1)} %get-tuple-element.6) | copy-start | bytes 3969028
  269.1 4.2 %copy-start.9 = (bf16[1088,608]{1,0:T(8,128)(2,1)S(1)}, bf16[1088,608]{1,0:T(8,128)(2,1)}, u32[]{:S(2)}) copy-start(bf16[1088,608]{1,0:T(8,128)(2,1)} %get-tuple-element.5) | copy-start | bytes 3969028
  273.3 2.5 copy-start.4
  273.3 2.5 copy-start.5
Sparse Core Ops, SparseCore 0:
  133.4 115.7 all-reduce.2
where the time goes:
time: 329 us; the launch traced here: 328 us
  waiting for transfers between devices  238 us (72%)
  starting transfers between devices  28.6 us (9%)
  matrix products  24.1 us (7%)
  local copies, waits for them, and re-layouts  17.6 us (5%)
  between operations  14.3 us (4%)
  other arithmetic  5.54 us (2%)
    psum x1, waiting for transfers between devices, on_device(): lax.psum(up_part.astype(jnp.bfloat16), 'tensor').astype(jnp.float32)  116 us
    all_to_all x1, waiting for transfers between devices, on_device(): lax.all_to_all(send_x, 'expert', split_axis=0, concat_axis=0, tiled=True)  43.2 us
    all_to_all x1, waiting for transfers between devices, on_device(): lax.all_to_all(send_grad, 'expert', split_axis=0, concat_axis=0, tiled=True)  39.9 us
    all_to_all x1, waiting for transfers between devices, on_device(): lax.all_to_all(partial_rows.reshape(devices, capacity, columns), 'expert'...  38.7 us
    all_to_all x1, starting transfers between devices, on_device(): lax.all_to_all(send_x, 'expert', split_axis=0, concat_axis=0, tiled=True)  11.8 us
    all_to_all x1, starting transfers between devices, on_device(): lax.all_to_all(partial_rows.reshape(devices, capacity, columns), 'expert'...  10.4 us
  transfers between devices with their start and end apart: 4, of which 4 were waited for; matrix products, arithmetic and copies ran while one was open for 7% of the time, Pallas kernels for 0%

commit v1 on v0

v1 whole, which is shorter than its diff:
```python
import jax
import jax.numpy as jnp
from jax import lax
from jax.sharding import PartitionSpec as P

MEMBERS = 4
CORES = 2
CAP = 17
MAIN = 16
SENT = 40
LANES = 128
BACK = 24


def activations(gate, up, grad_hidden):
    sigma = jax.nn.sigmoid(gate)
    silu = gate * sigma
    hidden = (silu * up).astype(jnp.bfloat16)
    grad_act_gate = (grad_hidden * up * sigma * (1.0 + gate * (1.0 - sigma))).astype(jnp.bfloat16)
    grad_act_up = (grad_hidden * silu).astype(jnp.bfloat16)
    return (hidden, grad_act_gate, grad_act_up)


def matmul(a, b, a_dim=1, b_dim=0):
    return lax.dot_general(
        a, b, (((a_dim,), (b_dim,)), ((), ())), preferred_element_type=jnp.float32
    )


def on_device(tokens, out_grad, expert_ids, gate_probs, w_gate, w_up, w_down):
    bf16 = jnp.bfloat16
    count, columns = tokens.shape
    devices = lax.axis_size("expert")
    chips = devices // CORES
    groups = devices // MEMBERS
    same_core = [[core + CORES * chip for chip in range(chips)] for core in range(CORES)]
    other_core = [(device, device ^ 1) for device in range(devices)]

    ids = expert_ids.T
    experts = jnp.arange(groups, dtype=jnp.int32)[:, None]
    first, second = ids[0][None, :] == experts, ids[1][None, :] == experts
    named = first | second
    before = (
        jnp.arange(count, dtype=jnp.int32)[:, None] < jnp.arange(count, dtype=jnp.int32)[None, :]
    )
    rank = matmul(named.astype(bf16), before.astype(bf16)).astype(jnp.int32)
    place = jnp.where(named, rank, -1)

    row = jnp.arange(SENT, dtype=jnp.int32)
    slot = jnp.where(row < 2 * MAIN, row % MAIN, MAIN)
    is_x = (row < MAIN) | (row == 2 * MAIN)
    is_grad = ((row >= MAIN) & (row < 2 * MAIN)) | (row == 2 * MAIN + 1)

    def chosen(mask, kind):
        hit = (jnp.where(mask, place, -1)[:, None, :] == slot[None, :, None]) & kind[None, :, None]
        hit = jnp.broadcast_to(hit[:, None], (groups, CORES, SENT, count))
        return hit.reshape(chips * SENT, count).astype(bf16)

    placing = jnp.concatenate(
        [chosen(named, is_x), chosen(first, is_grad), chosen(second, is_grad)], axis=1
    )
    wide = out_grad.astype(jnp.float32)
    rows = jnp.concatenate(
        [
            tokens,
            (wide * gate_probs[:, 0:1]).astype(bf16),
            (wide * gate_probs[:, 1:2]).astype(bf16),
        ],
        axis=0,
    )
    send = matmul(placing, rows).astype(bf16).reshape(chips, SENT, columns)
    mine = lax.all_to_all(
        send, "expert", split_axis=0, concat_axis=0, tiled=True, axis_index_groups=same_core
    )
    theirs = lax.ppermute(mine, "expert", other_core)

    half = chips * MAIN
    both = CORES * half

    def gathered(main, last):
        return jnp.concatenate(
            [
                mine[:, main : main + MAIN].reshape(half, columns),
                theirs[:, main : main + MAIN].reshape(half, columns),
                mine[:, last],
                theirs[:, last],
            ],
            axis=0,
        )

    local_x = gathered(0, 2 * MAIN)
    local_grad = gathered(MAIN, 2 * MAIN + 1)

    hidden_units = w_gate.shape[1]
    width = -(-hidden_units // LANES) * LANES
    pad = ((0, 0), (0, width - hidden_units))
    w_both = jnp.concatenate([jnp.pad(w_gate, pad), jnp.pad(w_up, pad)], axis=1)
    parts = jnp.concatenate(
        [
            matmul(local_x, w_both).astype(bf16),
            matmul(local_grad, jnp.pad(w_down, pad[::-1]), 1, 1).astype(bf16),
        ],
        axis=1,
    )
    sums = lax.psum_scatter(parts, "tensor", scatter_dimension=0, tiled=True).astype(jnp.float32)
    gate, up, grad_hidden = (sums[:, k * width : (k + 1) * width] for k in range(3))
    hidden, grad_act_gate, grad_act_up = activations(gate, up, grad_hidden)

    def spread(part):
        return lax.all_gather(part, "tensor", axis=0, tiled=True)

    cut = hidden_units - LANES
    most = spread(hidden[:, :cut])
    acts = spread(
        jnp.concatenate([grad_act_gate, grad_act_up, hidden[:, cut:hidden_units]], axis=1)
    )
    most, acts = lax.optimization_barrier((most, acts))
    acts, least = acts[:, : 2 * width], acts[:, 2 * width :]
    grad_down = jnp.concatenate(
        [matmul(part, local_grad, 0, 0).astype(bf16) for part in (most, least)], axis=0
    )
    grad_gate = matmul(local_x, acts[:, :hidden_units], 0, 0).astype(bf16)
    grad_up = matmul(local_x, acts[:, width : width + hidden_units], 0, 0).astype(bf16)

    partial = matmul(acts, w_both, 1, 1)
    away = jnp.concatenate([partial[half:both], partial[both + chips :]], axis=0).astype(bf16)
    here = jnp.concatenate([partial[:half], partial[both : both + chips]], axis=0)
    chip_rows = (here + lax.ppermute(away, "expert", other_core).astype(jnp.float32)).astype(bf16)
    back = jnp.concatenate(
        [
            chip_rows[:half].reshape(chips, MAIN, columns),
            chip_rows[half:][:, None],
            jnp.zeros((chips, BACK - CAP, columns), bf16),
        ],
        axis=1,
    )
    returned = lax.all_to_all(
        back, "expert", split_axis=0, concat_axis=0, tiled=True, axis_index_groups=same_core
    ).reshape(chips * BACK, columns)
    taking = place[:, None, None, :] == jnp.arange(BACK, dtype=jnp.int32)[None, None, :, None]
    taking = jnp.broadcast_to(taking, (groups, CORES, BACK, count)).reshape(chips * BACK, count)
    grad_tokens = matmul(taking.astype(bf16), returned, 0, 0).astype(bf16)
    return (grad_tokens, grad_gate, grad_up, grad_down)


def solution(mesh):
    placed = (
        P("expert", "tensor"),
        P("expert", "tensor"),
        P("expert", None),
        P("expert", None),
        P("tensor", "expert"),
        P("tensor", "expert"),
        P("expert", "tensor"),
    )
    return jax.shard_map(
        on_device,
        mesh=mesh,
        in_specs=placed,
        out_specs=(
            P("expert", "tensor"),
            P("tensor", "expert"),
            P("tensor", "expert"),
            P("expert", "tensor"),
        ),
        check_vma=False,
    )
```

time: 329 us -> 241 us (0.73)
  waiting for transfers between devices: 238 us -> 105 us
  blocking collectives: 0 us -> 71.1 us
  local copies, waits for them, and re-layouts: 17.6 us -> 3.01 us
  starting transfers between devices: 28.6 us -> 18.5 us
  matrix products: 24.1 us -> 17.8 us
    psum x1 -> x0, waiting for transfers between devices: 116 us -> none  [on_device(): lax.psum(up_part.astype(jnp.bfloat16), 'tensor').astype(jnp.float32)]
    all_to_all x3 -> x1, waiting for transfers between devices: 122 us -> 15.3 us  [on_device(): lax.all_to_all(back, 'expert', split_axis=0, concat_axis=0, tiled=True, a...]
    unnamed x1 -> x3, waiting for transfers between devices: 0.02 us -> 58.8 us
    all_to_all x0 -> x1, blocking collectives: none -> 47.8 us  [on_device(): lax.all_to_all(send, 'expert', split_axis=0, concat_axis=0, tiled=True, a...]
    all_gather x0 -> x1, waiting for transfers between devices: none -> 26.4 us  [spread(): return lax.all_gather(part, 'tensor', axis=0, tiled=True)]
    all_gather x0 -> x1, blocking collectives: none -> 23.3 us  [spread(): return lax.all_gather(part, 'tensor', axis=0, tiled=True)]
    all_to_all x3 -> x1, starting transfers between devices: 28.4 us -> 9.39 us  [on_device(): lax.all_to_all(back, 'expert', split_axis=0, concat_axis=0, tiled=True, a...]
    ppermute x0 -> x2, starting transfers between devices: none -> 9.04 us  [the longest x1 6.19 us: on_device(): theirs = lax.ppermute(mine, 'expert', other_core)]
  transfers between devices with their start and end apart: 4 -> 5, of which waited for: 4 -> 5; matrix products, arithmetic and copies ran while one was open for 7% -> 4% of each run, Pallas kernels for 0% -> 0%
where the time goes in v1:
time: 241 us; the launch traced here: 238 us
  waiting for transfers between devices  105 us (44%)
  blocking collectives  71.1 us (30%)
  starting transfers between devices  18.5 us (8%)
  matrix products  17.8 us (7%)
  between operations  14.5 us (6%)
  other arithmetic  8 us (3%)
  local copies, waits for them, and re-layouts  3.01 us (1%)
    unnamed x3, waiting for transfers between devices  58.8 us
    all_to_all x1, blocking collectives, on_device(): lax.all_to_all(send, 'expert', split_axis=0, concat_axis=0, tiled=True, a...  47.8 us
    all_gather x1, waiting for transfers between devices, spread(): return lax.all_gather(part, 'tensor', axis=0, tiled=True)  26.4 us
    all_gather x1, blocking collectives, spread(): return lax.all_gather(part, 'tensor', axis=0, tiled=True)  23.3 us
    dot_general x10, matrix products, matmul(): lax.dot_general(a, b, (((a_dim,), (b_dim,)), ((), ())), preferred_element...  17.8 us
    all_to_all x1, waiting for transfers between devices, on_device(): lax.all_to_all(back, 'expert', split_axis=0, concat_axis=0, tiled=True, a...  15.3 us
    all_to_all x1, starting transfers between devices, on_device(): lax.all_to_all(back, 'expert', split_axis=0, concat_axis=0, tiled=True, a...  9.39 us
    ppermute x1, starting transfers between devices, on_device(): theirs = lax.ppermute(mine, 'expert', other_core)  6.19 us
  transfers between devices with their start and end apart: 5, of which 5 were waited for; matrix products, arithmetic and copies ran while one was open for 4% of the time, Pallas kernels for 0%

profile of v1, /device:TPU:1, one launch (start us, length us, event | category | flops | bytes accessed | tf_op | source)
XLA Modules:
  0.0 237.8 jit_solution(7834419697692732359)
XLA Ops:
  7.2 0.8 slice_bitcast_fusion.4
  8.0 0.8 slice_bitcast_fusion.2
  8.8 0.1 fusion.30
  8.9 1.0 fusion.21
  9.9 0.2 and_convert_fusion.1
  10.4 1.1 convolution_convert_fusion.2
  11.5 47.8 %all_to_all.10 = bf16[32,40,640]{2,1,0:T(8,128)(2,1)S(1)} all-to-all(bf16[32,40,640]{2,1,0:T(8,128)(2,1)S(1)} %bitcast.40), channel_id=1, replica_groups={{0,16,32,48,64,80,96,112,128,144,160,176,192,208,224,240,256,272,288,30..., dimensions={0} | all-to-all | bytes 3276800 | tf_op jit(solution)/shard_map/all_to_all | solution.py:72
  59.2 6.2 %collective-permute-start = (bf16[32,40,640]{2,1,0:T(8,128)(2,1)S(1)}, bf16[32,40,640]{2,1,0:T(8,128)(2,1)S(1)}, u32[]{:S(2)}, u32[]{:S(2)}) collective-permute-start(bf16[32,40,640]{2,1,0:T(8,128)(2,1)S(1)} %all_to_all.10), channel_id=1, source_target_pairs={{0,8},{8,0},{16,24},{24,16},{32,40},{40,32},{48,56},{56,48},{64,72... | collective-permute-start | bytes 4915208 | tf_op jit(solution)/shard_map/ppermute | solution.py:75
  65.7 2.8 %collective-permute-done = bf16[32,40,640]{2,1,0:T(8,128)(2,1)S(1)} collective-permute-done((bf16[32,40,640]{2,1,0:T(8,128)(2,1)S(1)}, bf16[32,40,640]{2,1,0:T(8,128)(2,1)S(1)}, u32[]{:S(2)}, u32[]{:S(2)}) %collective-permute-start) | collective-permute-done | bytes 1638432 | tf_op jit(solution)/shard_map/ppermute | solution.py:75
  68.9 1.4 convolution_convert_fusion.1
  70.4 0.2 copy-done.11
  70.7 2.4 %convolution_convert_fusion = bf16[1088,1280]{1,0:T(8,128)(2,1)S(1)} fusion(bf16[640,608]{0,1:T(8,128)(2,1)S(1)} %copy-done.10, bf16[640,608]{0,1:T(8,128)(2,1)S(1)} %copy-done.11, bf16[32,640]{1,0:T(8,128)(2,1)S(1)} %bitcast.63, bf16[32,640]{1,0:T(8,128)(2,1)S(1)} %bitcast.57, bf16[512,640]{1,0:T(8,128)(2,1)S(1)} %bitcast.47, bf16[512,640]{1,0:T(8,128)(2,1)S(1)} %bitcast.41), kind=kOutput, calls=%fused_computation | convolution fusion | flops 1796096000 | bytes 5734400 | tf_op jit(solution)/shard_map/dot_general | solution.py:25
  73.1 2.3 pad_maximum_fusion
  75.4 58.8 %reduce-scatter.4.cloned.1.call-done = bf16[136,1920]{1,0:T(8,128)(2,1)} async-done(((bf16[1088,1920]{1,0:T(8,128)(2,1)}), bf16[136,1920]{1,0:T(8,128)(2,1)}) %reduce-scatter.4.cloned.1.call-update) | async-done | bytes 522256
  134.2 1.1 convert_element_type.97
  135.3 0.2 multiply_convert_fusion.1
  135.6 0.8 pad_maximum_fusion.5
  136.4 23.3 %all_gather.6 = bf16[1088,480]{1,0:T(8,128)(2,1)S(1)} all-gather(bf16[136,480]{1,0:T(8,128)(2,1)S(1)} %slice.122), channel_id=1, replica_groups=mesh['expert'=64,'tensor'=8] {'tensor'}, dimensions={0}, use_global_device_ids=true | all-gather | bytes 1175040 | tf_op jit(solution)/shard_map/all_gather | solution.py:110
  159.7 26.4 %all-gather.2.cloned.1.call-done = bf16[1088,1408]{1,0:T(8,128)(2,1)} async-done(((bf16[136,1408]{1,0:T(8,128)(2,1)}), bf16[1088,1408]{1,0:T(8,128)(2,1)}) %all-gather.2.cloned.1.call-update) | async-done | bytes 3063824 | tf_op jit(solution)/shard_map/all_gather | solution.py:110
  186.1 4.3 %fusion.45 = (bf16[1088,640]{1,0:T(8,128)(2,1)S(1)}, f32[1088,640]{1,0:T(8,128)S(1)}) fusion(bf16[640,608]{0,1:T(8,128)(2,1)S(1)} %copy-done.10, bf16[640,608]{0,1:T(8,128)(2,1)} %param.11, bf16[1088,1408]{1,0:T(8,128)(2,1)} %all-gather.2.cloned.1.call-done), kind=kOutput, calls=%fused_computation.88 | convolution fusion | flops 1789829120 | bytes 8519680 | tf_op jit(solution)/shard_map/dot_general | solution.py:25
  190.6 2.9 %collective-permute-start.1 = (bf16[544,640]{1,0:T(8,128)(2,1)S(1)}, bf16[544,640]{1,0:T(8,128)(2,1)S(1)}, u32[]{:S(2)}, u32[]{:S(2)}) collective-permute-start(bf16[544,640]{1,0:T(8,128)(2,1)S(1)} %pad_maximum_fusion.4), channel_id=1, source_target_pairs={{0,8},{8,0},{16,24},{24,16},{32,40},{40,32},{48,56},{56,48},{64,72... | collective-permute-start | bytes 2088968 | tf_op jit(solution)/shard_map/ppermute | solution.py:128
  193.7 1.6 collective-permute-done.1
  195.2 0.1 fusion.5
  195.5 1.2 maximum_maximum_fusion
  196.7 9.4 %all-to-all-start.1 = ((bf16[32,24,640]{2,1,0:T(8,128)(2,1)}), bf16[32,24,640]{2,1,0:T(8,128)(2,1)S(1)}, u32[]{:S(2)}, u32[]{:S(2)}) async-start(bf16[32,24,640]{2,1,0:T(8,128)(2,1)} %maximum_maximum_fusion), calls=%async_computation.1 | async-start | bytes 1966080 | tf_op jit(solution)/shard_map/all_to_all | solution.py:137
  206.2 1.7 convolution_convert_fusion.7
  208.0 1.1 convolution_convert_fusion.5
  209.1 0.9 pad_maximum_fusion.3
  210.1 2.3 convolution_convert_fusion.3
  212.4 2.3 convolution_convert_fusion.4
  214.6 15.3 %all-to-all-done.1 = bf16[32,24,640]{2,1,0:T(8,128)(2,1)S(1)} async-done(((bf16[32,24,640]{2,1,0:T(8,128)(2,1)}), bf16[32,24,640]{2,1,0:T(8,128)(2,1)S(1)}, u32[]{:S(2)}, u32[]{:S(2)}) %all-to-all-start.1) | async-done | bytes 983072 | tf_op jit(solution)/shard_map/all_to_all | solution.py:137
  229.9 1.0 convolution_convert_fusion.6
  (56 shorter events, 1.5 us)
Async XLA Ops:
  7.2 3.2 %copy-start.12 = (bf16[128,640]{1,0:T(8,128)(2,1)S(1)}, bf16[128,640]{1,0:T(8,128)(2,1)}, u32[]{:S(2)}) copy-start(bf16[128,640]{1,0:T(8,128)(2,1)} %param.7) | copy-start | bytes 491524
  7.2 127.0 %reduce-scatter.4.cloned.1.call-start = ((), (), s32[]{:S(2)}) async-start(), calls=%async_computation.4 | async-start | bytes 4700160
  59.2 9.3 %collective-permute-start = (bf16[32,40,640]{2,1,0:T(8,128)(2,1)S(1)}, bf16[32,40,640]{2,1,0:T(8,128)(2,1)S(1)}, u32[]{:S(2)}, u32[]{:S(2)}) collective-permute-start(bf16[32,40,640]{2,1,0:T(8,128)(2,1)S(1)} %all_to_all.10), channel_id=1, source_target_pairs={{0,8},{8,0},{16,24},{24,16},{32,40},{40,32},{48,56},{56,48},{64,72... | collective-permute-start | bytes 4915208 | tf_op jit(solution)/shard_map/ppermute | solution.py:75
  65.7 3.2 %copy-start.9 = (bf16[608,640]{1,0:T(8,128)(2,1)S(1)}, bf16[608,640]{1,0:T(8,128)(2,1)}, u32[]{:S(2)}) copy-start(bf16[608,640]{1,0:T(8,128)(2,1)} %param.13) | copy-start | bytes 2334724
  68.7 1.7 copy-start.4
  68.7 1.6 copy-start.6
  68.8 1.5 copy-start.2
  68.8 1.5 copy-start
  68.8 1.6 copy-start.10
  68.9 1.8 copy-start.11
  75.3 110.8 %all-gather.2.cloned.1.call-start = ((), (), s32[]{:S(2)}) async-start(), calls=%async_computation.3 | async-start | bytes 3446784 | tf_op jit(solution)/shard_map/all_gather | solution.py:110
  190.6 4.6 %collective-permute-start.1 = (bf16[544,640]{1,0:T(8,128)(2,1)S(1)}, bf16[544,640]{1,0:T(8,128)(2,1)S(1)}, u32[]{:S(2)}, u32[]{:S(2)}) collective-permute-start(bf16[544,640]{1,0:T(8,128)(2,1)S(1)} %pad_maximum_fusion.4), channel_id=1, source_target_pairs={{0,8},{8,0},{16,24},{24,16},{32,40},{40,32},{48,56},{56,48},{64,72... | collective-permute-start | bytes 2088968 | tf_op jit(solution)/shard_map/ppermute | solution.py:128
  196.7 33.2 %all-to-all-start.1 = ((bf16[32,24,640]{2,1,0:T(8,128)(2,1)}), bf16[32,24,640]{2,1,0:T(8,128)(2,1)S(1)}, u32[]{:S(2)}, u32[]{:S(2)}) async-start(bf16[32,24,640]{2,1,0:T(8,128)(2,1)} %maximum_maximum_fusion), calls=%async_computation.1 | async-start | bytes 1966080 | tf_op jit(solution)/shard_map/all_to_all | solution.py:137
  206.2 1.7 copy-start.3
  206.2 1.7 copy-start.7
  207.9 2.1 copy-start.1
  208.0 2.1 copy-start.5
  208.0 2.1 copy-start.8
Sparse Core Ops, SparseCore 0:
  75.5 58.6 reduce-scatter.3
  136.8 49.2 all-gather.1

commit v2 on v1

v2 whole, which is shorter than its diff:
```python
import jax
import jax.numpy as jnp
from jax import lax
from jax.sharding import PartitionSpec as P

MEMBERS = 4
CORES = 2
MAIN = 16
SUBLANES = 8
LANES = 128


def activations(gate, up, grad_hidden):
    sigma = jax.nn.sigmoid(gate)
    silu = gate * sigma
    hidden = (silu * up).astype(jnp.bfloat16)
    grad_act_gate = (grad_hidden * up * sigma * (1.0 + gate * (1.0 - sigma))).astype(jnp.bfloat16)
    grad_act_up = (grad_hidden * silu).astype(jnp.bfloat16)
    return (hidden, grad_act_gate, grad_act_up)


def matmul(a, b, a_dim=1, b_dim=0):
    return lax.dot_general(
        a, b, (((a_dim,), (b_dim,)), ((), ())), preferred_element_type=jnp.float32
    )


def on_device(tokens, out_grad, expert_ids, gate_probs, w_gate, w_up, w_down):
    bf16 = jnp.bfloat16
    count, columns = tokens.shape
    devices = lax.axis_size("expert")
    chips = devices // CORES
    groups = devices // MEMBERS
    same_core = [[core + CORES * chip for chip in range(chips)] for core in range(CORES)]
    other_core = [(device, device ^ 1) for device in range(devices)]

    ids = expert_ids.T
    experts = jnp.arange(groups, dtype=jnp.int32)[:, None]
    first, second = ids[0][None, :] == experts, ids[1][None, :] == experts
    named = first | second
    before = (
        jnp.arange(count, dtype=jnp.int32)[:, None] < jnp.arange(count, dtype=jnp.int32)[None, :]
    )
    rank = matmul(named.astype(bf16), before.astype(bf16)).astype(jnp.int32)
    place = jnp.where(named, rank, -1)

    main_slot = jnp.arange(MAIN, dtype=jnp.int32)[None, :, None]

    def chosen(mask):
        held = jnp.where(mask, place, -1)
        main = jnp.broadcast_to(
            (held[:, None, :] == main_slot)[:, None], (groups, CORES, MAIN, count)
        ).reshape(chips * MAIN, count)
        last = jnp.broadcast_to((held == MAIN)[:, None], (groups, CORES, count))
        return main.astype(bf16), last.reshape(chips, count).astype(bf16)

    blocks = columns // LANES
    tiles = MAIN // SUBLANES

    def fold(main, last):
        main = main.reshape(chips, tiles, SUBLANES, blocks, LANES).transpose(0, 1, 3, 2, 4)
        main = main.reshape(chips, MAIN * blocks, LANES)
        last = last.reshape(chips, blocks, LANES)
        spare = jnp.zeros((chips, -blocks % SUBLANES, LANES), last.dtype)
        return jnp.concatenate([main, last, spare], axis=1)

    def unfold(rows):
        main = rows[:, : MAIN * blocks].reshape(chips, tiles, blocks, SUBLANES, LANES)
        main = main.transpose(0, 1, 3, 2, 4).reshape(chips * MAIN, columns)
        return main, rows[:, MAIN * blocks : MAIN * blocks + blocks].reshape(chips, columns)

    def exchange(rows):
        return lax.all_to_all(
            rows, "expert", split_axis=0, concat_axis=0, tiled=True, axis_index_groups=same_core
        )

    def routed(send):
        mine = exchange(send)
        theirs = lax.ppermute(mine, "expert", other_core)
        (main_a, last_a), (main_b, last_b) = unfold(mine), unfold(theirs)
        return jnp.concatenate([main_a, main_b, last_a, last_b], axis=0)

    half = chips * MAIN
    both = CORES * half
    send_x = fold(*(matmul(part, tokens).astype(bf16) for part in chosen(named)))
    wide = out_grad.astype(jnp.float32)
    scaled = jnp.concatenate(
        [
            (wide * gate_probs[:, 0:1]).astype(bf16),
            (wide * gate_probs[:, 1:2]).astype(bf16),
        ],
        axis=0,
    )
    send_grad = fold(
        *(
            matmul(jnp.concatenate(pair, axis=1), scaled).astype(bf16)
            for pair in zip(chosen(first), chosen(second), strict=True)
        )
    )
    local_x = routed(send_x)

    hidden_units = w_gate.shape[1]
    width = -(-hidden_units // LANES) * LANES
    pad = ((0, 0), (0, width - hidden_units))
    w_both = jnp.concatenate([jnp.pad(w_gate, pad), jnp.pad(w_up, pad)], axis=1)
    parts = matmul(local_x, w_both).astype(bf16)
    parts, send_grad = lax.optimization_barrier((parts, send_grad))
    sums = lax.psum_scatter(parts, "tensor", scatter_dimension=0, tiled=True).astype(jnp.float32)
    gate, up = sums[:, :width], sums[:, width:]

    local_grad = routed(send_grad)
    shards = lax.axis_size("tensor")
    pieces = matmul(local_grad, jnp.pad(w_down, pad[::-1]), 1, 1).astype(bf16)
    pieces = lax.all_to_all(
        pieces.reshape(shards, pieces.shape[0] // shards, width),
        "tensor",
        split_axis=0,
        concat_axis=0,
        tiled=True,
    )
    grad_hidden = jnp.sum(pieces.astype(jnp.float32), axis=0)
    hidden, grad_act_gate, grad_act_up = activations(gate, up, grad_hidden)

    def spread(part):
        return lax.all_gather(part, "tensor", axis=0, tiled=True)

    cut = hidden_units - LANES
    most = spread(hidden[:, :cut])
    acts = spread(
        jnp.concatenate([grad_act_gate, grad_act_up, hidden[:, cut:hidden_units]], axis=1)
    )
    most, acts = lax.optimization_barrier((most, acts))
    acts, least = acts[:, : 2 * width], acts[:, 2 * width :]
    grad_down = jnp.concatenate(
        [matmul(part, local_grad, 0, 0).astype(bf16) for part in (most, least)], axis=0
    )
    grad_gate = matmul(local_x, acts[:, :hidden_units], 0, 0).astype(bf16)
    grad_up = matmul(local_x, acts[:, width : width + hidden_units], 0, 0).astype(bf16)

    partial = matmul(acts, w_both, 1, 1)
    away = jnp.concatenate([partial[half:both], partial[both + chips :]], axis=0).astype(bf16)
    here = jnp.concatenate([partial[:half], partial[both : both + chips]], axis=0)
    chip_rows = (here + lax.ppermute(away, "expert", other_core).astype(jnp.float32)).astype(bf16)
    returned = jnp.concatenate(unfold(exchange(fold(chip_rows[:half], chip_rows[half:]))), axis=0)
    taking = jnp.concatenate(chosen(named), axis=0)
    grad_tokens = matmul(taking, returned, 0, 0).astype(bf16)
    return (grad_tokens, grad_gate, grad_up, grad_down)


def solution(mesh):
    placed = (
        P("expert", "tensor"),
        P("expert", "tensor"),
        P("expert", None),
        P("expert", None),
        P("tensor", "expert"),
        P("tensor", "expert"),
        P("expert", "tensor"),
    )
    return jax.shard_map(
        on_device,
        mesh=mesh,
        in_specs=placed,
        out_specs=(
            P("expert", "tensor"),
            P("tensor", "expert"),
            P("tensor", "expert"),
            P("expert", "tensor"),
        ),
        check_vma=False,
    )
```

time: 241 us -> 230 us (0.954)
  waiting for transfers between devices: 105 us -> 38.3 us
  blocking collectives: 71.1 us -> 121 us
  starting transfers between devices: 18.5 us -> 24.1 us
    unnamed x3 -> x2, waiting for transfers between devices: 58.8 us -> 0.03 us
    all_to_all x1 -> x3, blocking collectives: 47.8 us -> 95.9 us  [the longest x2 50.8 us: exchange(): lax.all_to_all(rows, 'expert', split_axis=0, concat_axis=0, tiled=True, a...]
    ppermute x1 -> x2, starting transfers between devices: 6.19 us -> 13.2 us  [routed(): theirs = lax.ppermute(mine, 'expert', other_core)]
    all_to_all x1, waiting for transfers between devices: 15.3 us -> 8.96 us  [exchange(): lax.all_to_all(rows, 'expert', split_axis=0, concat_axis=0, tiled=True, a...]
    dot_general x10 -> x13, matrix products: 17.8 us -> 19.7 us  [matmul(): lax.dot_general(a, b, (((a_dim,), (b_dim,)), ((), ())), preferred_element...]
  transfers between devices with their start and end apart: 5 -> 6, of which waited for: 5 -> 5; matrix products, arithmetic and copies ran while one was open for 4% -> 5% of each run, Pallas kernels for 0% -> 0%
where the time goes in v2:
time: 230 us; the launch traced here: 226 us
  blocking collectives  121 us (53%)
  waiting for transfers between devices  38.3 us (17%)
  starting transfers between devices  24.1 us (10%)
  matrix products  19.7 us (9%)
  between operations  14.5 us (6%)
  other arithmetic  5.89 us (3%)
  local copies, waits for them, and re-layouts  2.61 us (1%)
    all_to_all x2, blocking collectives, exchange(): lax.all_to_all(rows, 'expert', split_axis=0, concat_axis=0, tiled=True, a...  50.8 us
    all_to_all x1, blocking collectives, on_device(): lax.all_to_all(pieces.reshape(shards, pieces.shape[0] // shards, width),...  45.1 us
    all_gather x1, blocking collectives, spread(): return lax.all_gather(part, 'tensor', axis=0, tiled=True)  24.9 us
    all_gather x1, waiting for transfers between devices, spread(): return lax.all_gather(part, 'tensor', axis=0, tiled=True)  24.3 us
    dot_general x13, matrix products, matmul(): lax.dot_general(a, b, (((a_dim,), (b_dim,)), ((), ())), preferred_element...  19.7 us
    ppermute x2, starting transfers between devices, routed(): theirs = lax.ppermute(mine, 'expert', other_core)  13.2 us
    all_to_all x1, waiting for transfers between devices, exchange(): lax.all_to_all(rows, 'expert', split_axis=0, concat_axis=0, tiled=True, a...  8.96 us
    all_to_all x1, starting transfers between devices, exchange(): lax.all_to_all(rows, 'expert', split_axis=0, concat_axis=0, tiled=True, a...  8.29 us
  transfers between devices with their start and end apart: 6, of which 5 were waited for; matrix products, arithmetic and copies ran while one was open for 5% of the time, Pallas kernels for 0%

profile of v2, /device:TPU:1, one launch (start us, length us, event | category | flops | bytes accessed | tf_op | source)
XLA Modules:
  0.0 226.0 jit_solution(5333331569617336635)
XLA Ops:
  7.2 0.8 slice_bitcast_fusion.3
  8.0 0.8 slice_bitcast_fusion.1
  9.2 1.0 fusion.14
  10.6 0.3 convolution_convert_fusion.4
  11.1 0.4 convolution_convert_fusion.5
  11.4 0.4 maximum_maximum_fusion.1
  11.8 28.7 %all_to_all.20 = bf16[32,88,128]{2,1,0:T(8,128)(2,1)S(1)} all-to-all(bf16[32,88,128]{2,1,0:T(8,128)(2,1)S(1)} %get-tuple-element.32), channel_id=1, replica_groups={{0,16,32,48,64,80,96,112,128,144,160,176,192,208,224,240,256,272,288,30..., dimensions={0} | all-to-all | bytes 1441792 | tf_op jit(solution)/shard_map/all_to_all | solution.py:73
  40.5 6.4 %collective-permute-start = (bf16[32,88,128]{2,1,0:T(8,128)(2,1)S(1)}, bf16[32,88,128]{2,1,0:T(8,128)(2,1)S(1)}, u32[]{:S(2)}, u32[]{:S(2)}) collective-permute-start(bf16[32,88,128]{2,1,0:T(8,128)(2,1)S(1)} %all_to_all.20), channel_id=1, source_target_pairs={{0,8},{8,0},{16,24},{24,16},{32,40},{40,32},{48,56},{56,48},{64,72... | collective-permute-start | bytes 2162696 | tf_op jit(solution)/shard_map/ppermute | solution.py:79
  47.0 1.7 collective-permute-done
  48.8 3.9 %convolution_convert_fusion = bf16[1088,1280]{1,0:T(8,128)(2,1)} fusion(bf16[640,608]{0,1:T(8,128)(2,1)S(1)} %copy-done.9, bf16[640,608]{0,1:T(8,128)(2,1)S(1)} %copy-done.10, bf16[32,640]{1,0:T(8,128)(2,1)S(1)} %bitcast.109, bf16[32,640]{1,0:T(8,128)(2,1)S(1)} %bitcast.106, bf16[512,640]{1,0:T(8,128)(2,1)S(1)} %bitcast.86, bf16[512,640]{1,0:T(8,128)(2,1)S(1)} %bitcast.83), kind=kOutput, calls=%fused_computation | convolution fusion | flops 1796096000 | bytes 5734400 | tf_op jit(solution)/shard_map/dot_general | solution.py:23
  52.9 22.1 %all_to_all.21 = bf16[32,88,128]{2,1,0:T(8,128)(2,1)S(1)} all-to-all(bf16[32,88,128]{2,1,0:T(8,128)(2,1)S(1)} %get-tuple-element.9), channel_id=1, replica_groups={{0,16,32,48,64,80,96,112,128,144,160,176,192,208,224,240,256,272,288,30..., dimensions={0} | all-to-all | bytes 1441792 | tf_op jit(solution)/shard_map/all_to_all | solution.py:73
  75.0 6.7 %collective-permute-start.1 = (bf16[32,88,128]{2,1,0:T(8,128)(2,1)S(1)}, bf16[32,88,128]{2,1,0:T(8,128)(2,1)S(1)}, u32[]{:S(2)}, u32[]{:S(2)}) collective-permute-start(bf16[32,88,128]{2,1,0:T(8,128)(2,1)S(1)} %all_to_all.21), channel_id=1, source_target_pairs={{0,8},{8,0},{16,24},{24,16},{32,40},{40,32},{48,56},{56,48},{64,72... | collective-permute-start | bytes 2162696 | tf_op jit(solution)/shard_map/ppermute | solution.py:79
  81.8 1.7 collective-permute-done.1
  83.6 1.4 convolution_convert_fusion.1
  85.1 45.1 %all_to_all.22 = bf16[8,136,640]{2,1,0:T(8,128)(2,1)S(1)} all-to-all(bf16[8,136,640]{2,1,0:T(8,128)(2,1)S(1)} %bitcast.82), channel_id=1, replica_groups=mesh['expert'=64,'tensor'=8] {'tensor'}, dimensions={0} | all-to-all | bytes 2785280 | tf_op jit(solution)/shard_map/all_to_all | solution.py:114
  130.4 1.0 convert_element_type.123
  131.4 0.2 multiply_convert_fusion.1
  131.8 0.8 pad_maximum_fusion.4
  132.6 24.9 %all_gather.6 = bf16[1088,480]{1,0:T(8,128)(2,1)S(1)} all-gather(bf16[136,480]{1,0:T(8,128)(2,1)S(1)} %slice.122), channel_id=1, replica_groups=mesh['expert'=64,'tensor'=8] {'tensor'}, dimensions={0}, use_global_device_ids=true | all-gather | bytes 1175040 | tf_op jit(solution)/shard_map/all_gather | solution.py:125
  157.5 24.3 %all-gather.2.cloned.1.call-done = bf16[1088,1408]{1,0:T(8,128)(2,1)} async-done(((bf16[136,1408]{1,0:T(8,128)(2,1)}), bf16[1088,1408]{1,0:T(8,128)(2,1)}) %all-gather.2.cloned.1.call-update) | async-done | bytes 3063824 | tf_op jit(solution)/shard_map/all_gather | solution.py:125
  181.8 4.5 %fusion.51 = (bf16[1088,640]{1,0:T(8,128)(2,1)S(1)}, f32[1088,640]{1,0:T(8,128)S(1)}) fusion(bf16[640,608]{0,1:T(8,128)(2,1)} %param.12, bf16[640,608]{0,1:T(8,128)(2,1)} %param.11, bf16[1088,1408]{1,0:T(8,128)(2,1)} %all-gather.2.cloned.1.call-done), kind=kOutput, calls=%fused_computation.94 | convolution fusion | flops 1789829120 | bytes 8519680 | tf_op jit(solution)/shard_map/dot_general | solution.py:23
  186.5 2.6 %collective-permute-start.2 = (bf16[544,640]{1,0:T(8,128)(2,1)S(1)}, bf16[544,640]{1,0:T(8,128)(2,1)S(1)}, u32[]{:S(2)}, u32[]{:S(2)}) collective-permute-start(bf16[544,640]{1,0:T(8,128)(2,1)S(1)} %pad_maximum_fusion.3), channel_id=1, source_target_pairs={{0,8},{8,0},{16,24},{24,16},{32,40},{40,32},{48,56},{56,48},{64,72... | collective-permute-start | bytes 2088968 | tf_op jit(solution)/shard_map/ppermute | solution.py:143
  189.2 1.7 collective-permute-done.2
  191.1 1.1 maximum_maximum_fusion.2
  192.2 8.3 %all-to-all-start.3 = ((bf16[32,88,128]{2,1,0:T(8,128)(2,1)}), bf16[32,88,128]{2,1,0:T(8,128)(2,1)S(1)}, u32[]{:S(2)}, u32[]{:S(2)}) async-start(bf16[32,88,128]{2,1,0:T(8,128)(2,1)} %maximum_maximum_fusion.2), calls=%async_computation.4 | async-start | bytes 1441792 | tf_op jit(solution)/shard_map/all_to_all | solution.py:73
  200.5 1.9 convolution_convert_fusion.8
  202.5 1.1 convolution_convert_fusion.6
  203.6 0.9 pad_maximum_fusion.2
  204.6 2.3 %convolution_convert_fusion.2 = bf16[640,608]{0,1:T(8,128)(2,1)} fusion(bf16[1088,1408]{1,0:T(8,128)(2,1)S(1)} %copy-done.7, bf16[32,640]{1,0:T(8,128)(2,1)S(1)} %bitcast.110, bf16[32,640]{1,0:T(8,128)(2,1)S(1)} %bitcast.107, bf16[512,640]{1,0:T(8,128)(2,1)S(1)} %bitcast.87, bf16[512,640]{1,0:T(8,128)(2,1)S(1)} %bitcast.84), kind=kOutput, calls=%fused_computation.10 | convolution fusion | flops 852684800 | bytes 3563520 | tf_op jit(solution)/shard_map/dot_general | solution.py:23
  206.9 2.3 %convolution_convert_fusion.3 = bf16[640,608]{0,1:T(8,128)(2,1)} fusion(bf16[1088,1408]{1,0:T(8,128)(2,1)S(1)} %copy-done.7, bf16[32,640]{1,0:T(8,128)(2,1)S(1)} %bitcast.111, bf16[32,640]{1,0:T(8,128)(2,1)S(1)} %bitcast.108, bf16[512,640]{1,0:T(8,128)(2,1)S(1)} %bitcast.88, bf16[512,640]{1,0:T(8,128)(2,1)S(1)} %bitcast.85), kind=kOutput, calls=%fused_computation.11 | convolution fusion | flops 852684800 | bytes 3563520 | tf_op jit(solution)/shard_map/dot_general | solution.py:23
  209.1 9.0 %all-to-all-done.3 = bf16[32,88,128]{2,1,0:T(8,128)(2,1)S(1)} async-done(((bf16[32,88,128]{2,1,0:T(8,128)(2,1)}), bf16[32,88,128]{2,1,0:T(8,128)(2,1)S(1)}, u32[]{:S(2)}, u32[]{:S(2)}) %all-to-all-start.3) | async-done | bytes 720928 | tf_op jit(solution)/shard_map/all_to_all | solution.py:73
  218.2 1.0 convolution_convert_fusion.7
  (70 shorter events, 2.1 us)
Async XLA Ops:
  7.2 1.8 copy-start
  7.2 123.2 %reduce-scatter.2.cloned.1.call-start = ((), (), s32[]{:S(2)}) async-start(), calls=%async_computation.5 | async-start | bytes 3133440 | tf_op jit(solution)/shard_map/reduce_scatter | solution.py:108
  40.5 8.3 %copy-start.9 = (bf16[640,608]{0,1:T(8,128)(2,1)S(1)}, bf16[640,608]{0,1:T(8,128)(2,1)}, u32[]{:S(2)}) copy-start(bf16[640,608]{0,1:T(8,128)(2,1)} %param.12) | copy-start | bytes 2334724
  40.5 8.3 %copy-start.10 = (bf16[640,608]{0,1:T(8,128)(2,1)S(1)}, bf16[640,608]{0,1:T(8,128)(2,1)}, u32[]{:S(2)}) copy-start(bf16[640,608]{0,1:T(8,128)(2,1)} %param.11) | copy-start | bytes 2334724
  40.5 8.2 %collective-permute-start = (bf16[32,88,128]{2,1,0:T(8,128)(2,1)S(1)}, bf16[32,88,128]{2,1,0:T(8,128)(2,1)S(1)}, u32[]{:S(2)}, u32[]{:S(2)}) collective-permute-start(bf16[32,88,128]{2,1,0:T(8,128)(2,1)S(1)} %all_to_all.20), channel_id=1, source_target_pairs={{0,8},{8,0},{16,24},{24,16},{32,40},{40,32},{48,56},{56,48},{64,72... | collective-permute-start | bytes 2162696 | tf_op jit(solution)/shard_map/ppermute | solution.py:79
  52.8 129.0 %all-gather.2.cloned.1.call-start = ((), (), s32[]{:S(2)}) async-start(), calls=%async_computation.6 | async-start | bytes 3446784 | tf_op jit(solution)/shard_map/all_gather | solution.py:125
  75.0 8.6 %copy-start.8 = (bf16[608,640]{1,0:T(8,128)(2,1)S(1)}, bf16[608,640]{1,0:T(8,128)(2,1)}, u32[]{:S(2)}) copy-start(bf16[608,640]{1,0:T(8,128)(2,1)} %param.13) | copy-start | bytes 2334724
  75.0 8.5 %collective-permute-start.1 = (bf16[32,88,128]{2,1,0:T(8,128)(2,1)S(1)}, bf16[32,88,128]{2,1,0:T(8,128)(2,1)S(1)}, u32[]{:S(2)}, u32[]{:S(2)}) collective-permute-start(bf16[32,88,128]{2,1,0:T(8,128)(2,1)S(1)} %all_to_all.21), channel_id=1, source_target_pairs={{0,8},{8,0},{16,24},{24,16},{32,40},{40,32},{48,56},{56,48},{64,72... | collective-permute-start | bytes 2162696 | tf_op jit(solution)/shard_map/ppermute | solution.py:79
  81.8 3.3 %copy-start.1 = (bf16[32,80,128]{2,1,0:T(8,128)(2,1)}, bf16[32,80,128]{2,1,0:T(8,128)(2,1)S(1)}, u32[]{:S(2)}) copy-start(bf16[32,80,128]{2,1,0:T(8,128)(2,1)S(1)} %slice.123) | copy-start | bytes 1966084
  83.6 1.5 copy-start.5
  83.6 1.5 copy-start.3
  186.5 4.4 %collective-permute-start.2 = (bf16[544,640]{1,0:T(8,128)(2,1)S(1)}, bf16[544,640]{1,0:T(8,128)(2,1)S(1)}, u32[]{:S(2)}, u32[]{:S(2)}) collective-permute-start(bf16[544,640]{1,0:T(8,128)(2,1)S(1)} %pad_maximum_fusion.3), channel_id=1, source_target_pairs={{0,8},{8,0},{16,24},{24,16},{32,40},{40,32},{48,56},{56,48},{64,72... | collective-permute-start | bytes 2088968 | tf_op jit(solution)/shard_map/ppermute | solution.py:143
  191.1 9.4 %copy-start.6 = (bf16[4,8,5,128]{3,1,2,0:T(8,128)(2,1)S(1)}, bf16[4,8,5,128]{3,1,2,0:T(8,128)(2,1)}, u32[]{:S(2)}) copy-start(bf16[4,8,5,128]{3,1,2,0:T(8,128)(2,1)} %copy-done.5) | copy-start | bytes 122884
  192.2 25.9 %all-to-all-start.3 = ((bf16[32,88,128]{2,1,0:T(8,128)(2,1)}), bf16[32,88,128]{2,1,0:T(8,128)(2,1)S(1)}, u32[]{:S(2)}, u32[]{:S(2)}) async-start(bf16[32,88,128]{2,1,0:T(8,128)(2,1)} %maximum_maximum_fusion.2), calls=%async_computation.4 | async-start | bytes 1441792 | tf_op jit(solution)/shard_map/all_to_all | solution.py:73
  200.5 2.0 copy-start.2
  200.5 2.0 copy-start.4
  202.5 2.1 copy-start.7
Sparse Core Ops, SparseCore 0:
  52.9 43.9 reduce-scatter.1
  132.7 49.0 all-gather.1

commit v3 on v2

--- a/solution.py
+++ b/solution.py
@@ -78,11 +78,12 @@
         mine = exchange(send)
         theirs = lax.ppermute(mine, "expert", other_core)
         (main_a, last_a), (main_b, last_b) = unfold(mine), unfold(theirs)
-        return jnp.concatenate([main_a, main_b, last_a, last_b], axis=0)
+        return jnp.concatenate([main_a, last_a, main_b, last_b], axis=0)
 
-    half = chips * MAIN
-    both = CORES * half
+    main = chips * MAIN
+    half = main + chips
     send_x = fold(*(matmul(part, tokens).astype(bf16) for part in chosen(named)))
+    send_x, out_grad, gate_probs = lax.optimization_barrier((send_x, out_grad, gate_probs))
     wide = out_grad.astype(jnp.float32)
     scaled = jnp.concatenate(
         [
@@ -105,8 +106,8 @@
     w_both = jnp.concatenate([jnp.pad(w_gate, pad), jnp.pad(w_up, pad)], axis=1)
     parts = matmul(local_x, w_both).astype(bf16)
     parts, send_grad = lax.optimization_barrier((parts, send_grad))
-    sums = lax.psum_scatter(parts, "tensor", scatter_dimension=0, tiled=True).astype(jnp.float32)
-    gate, up = sums[:, :width], sums[:, width:]
+    sums = lax.psum_scatter(parts, "tensor", scatter_dimension=0, tiled=True)
+    gate, up = (sums[:, k * width : (k + 1) * width].astype(jnp.float32) for k in range(2))
 
     local_grad = routed(send_grad)
     shards = lax.axis_size("tensor")
@@ -137,11 +138,12 @@
     grad_gate = matmul(local_x, acts[:, :hidden_units], 0, 0).astype(bf16)
     grad_up = matmul(local_x, acts[:, width : width + hidden_units], 0, 0).astype(bf16)
 
-    partial = matmul(acts, w_both, 1, 1)
-    away = jnp.concatenate([partial[half:both], partial[both + chips :]], axis=0).astype(bf16)
-    here = jnp.concatenate([partial[:half], partial[both : both + chips]], axis=0)
-    chip_rows = (here + lax.ppermute(away, "expert", other_core).astype(jnp.float32)).astype(bf16)
-    returned = jnp.concatenate(unfold(exchange(fold(chip_rows[:half], chip_rows[half:]))), axis=0)
+    away = matmul(acts[half:], w_both, 1, 1).astype(bf16)
+    away, acts = lax.optimization_barrier((away, acts))
+    here = lax.optimization_barrier(matmul(acts[:half], w_both, 1, 1))
+    away = lax.ppermute(away, "expert", other_core)
+    chip_rows = (here + away.astype(jnp.float32)).astype(bf16)
+    returned = jnp.concatenate(unfold(exchange(fold(chip_rows[:main], chip_rows[main:]))), axis=0)
     taking = jnp.concatenate(chosen(named), axis=0)
     grad_tokens = matmul(taking, returned, 0, 0).astype(bf16)
     return (grad_tokens, grad_gate, grad_up, grad_down)

time: 230 us -> 228 us (level)
  blocking collectives: 121 us -> 91.9 us
  waiting for transfers between devices: 38.3 us -> 54.5 us
  starting transfers between devices: 24.1 us -> 34.9 us
    all_to_all x2 -> x1, blocking collectives: 50.8 us -> 22.2 us  [exchange(): lax.all_to_all(rows, 'expert', split_axis=0, concat_axis=0, tiled=True, a...]
    all_to_all x1 -> x2, waiting for transfers between devices: 8.96 us -> 27.2 us  [exchange(): lax.all_to_all(rows, 'expert', split_axis=0, concat_axis=0, tiled=True, a...]
    all_to_all x1 -> x2, starting transfers between devices: 8.29 us -> 19 us  [exchange(): lax.all_to_all(rows, 'expert', split_axis=0, concat_axis=0, tiled=True, a...]
    dot_general x13 -> x14, matrix products: 19.7 us -> 19.4 us  [matmul(): lax.dot_general(a, b, (((a_dim,), (b_dim,)), ((), ())), preferred_element...]
  transfers between devices with their start and end apart: 6 -> 7, of which waited for: 5 -> 6; matrix products, arithmetic and copies ran while one was open for 5% -> 6% of each run, Pallas kernels for 0% -> 0%
where the time goes in v3:
time: 228 us; the launch traced here: 224 us
  blocking collectives  91.9 us (40%)
  waiting for transfers between devices  54.5 us (24%)
  starting transfers between devices  34.9 us (15%)
  matrix products  19.4 us (9%)
  between operations  14.6 us (6%)
  other arithmetic  5.78 us (3%)
  local copies, waits for them, and re-layouts  2.56 us (1%)
    all_to_all x1, blocking collectives, on_device(): lax.all_to_all(pieces.reshape(shards, pieces.shape[0] // shards, width),...  44.8 us
    all_to_all x2, waiting for transfers between devices, exchange(): lax.all_to_all(rows, 'expert', split_axis=0, concat_axis=0, tiled=True, a...  27.2 us
    all_gather x1, blocking collectives, spread(): return lax.all_gather(part, 'tensor', axis=0, tiled=True)  24.9 us
    all_gather x1, waiting for transfers between devices, spread(): return lax.all_gather(part, 'tensor', axis=0, tiled=True)  24.5 us
    all_to_all x1, blocking collectives, exchange(): lax.all_to_all(rows, 'expert', split_axis=0, concat_axis=0, tiled=True, a...  22.2 us
    dot_general x14, matrix products, matmul(): lax.dot_general(a, b, (((a_dim,), (b_dim,)), ((), ())), preferred_element...  19.4 us
    all_to_all x2, starting transfers between devices, exchange(): lax.all_to_all(rows, 'expert', split_axis=0, concat_axis=0, tiled=True, a...  19 us
    ppermute x2, starting transfers between devices, routed(): theirs = lax.ppermute(mine, 'expert', other_core)  13 us
  transfers between devices with their start and end apart: 7, of which 6 were waited for; matrix products, arithmetic and copies ran while one was open for 6% of the time, Pallas kernels for 0%

profile of v3, /device:TPU:1, one launch (start us, length us, event | category | flops | bytes accessed | tf_op | source)
XLA Modules:
  0.0 223.7 jit_solution(2378944772460016975)
XLA Ops:
  7.2 0.8 slice_bitcast_fusion.3
  8.4 0.3 convolution_convert_fusion.4
  8.9 1.1 maximum_maximum_fusion
  10.0 10.5 %all-to-all-start = ((bf16[32,88,128]{2,1,0:T(8,128)(2,1)}), bf16[32,88,128]{2,1,0:T(8,128)(2,1)S(1)}, u32[]{:S(2)}, u32[]{:S(2)}) async-start(bf16[32,88,128]{2,1,0:T(8,128)(2,1)} %maximum_maximum_fusion), calls=%async_computation | async-start | bytes 1441792 | tf_op jit(solution)/shard_map/all_to_all | solution.py:73
  20.5 18.3 %all-to-all-done = bf16[32,88,128]{2,1,0:T(8,128)(2,1)S(1)} async-done(((bf16[32,88,128]{2,1,0:T(8,128)(2,1)}), bf16[32,88,128]{2,1,0:T(8,128)(2,1)S(1)}, u32[]{:S(2)}, u32[]{:S(2)}) %all-to-all-start) | async-done | bytes 720928 | tf_op jit(solution)/shard_map/all_to_all | solution.py:73
  38.9 6.3 %collective-permute-start = (bf16[32,88,128]{2,1,0:T(8,128)(2,1)S(1)}, bf16[32,88,128]{2,1,0:T(8,128)(2,1)S(1)}, u32[]{:S(2)}, u32[]{:S(2)}) collective-permute-start(bf16[32,88,128]{2,1,0:T(8,128)(2,1)S(1)} %all-to-all-done), channel_id=1, source_target_pairs={{0,8},{8,0},{16,24},{24,16},{32,40},{40,32},{48,56},{56,48},{64,72... | collective-permute-start | bytes 2162696 | tf_op jit(solution)/shard_map/ppermute | solution.py:79
  45.6 0.4 convolution_convert_fusion.5
  46.3 0.6 collective-permute-done
  47.0 0.8 copy-done.2
  47.8 3.9 %convolution_convert_fusion = bf16[1088,1280]{1,0:T(8,128)(2,1)} fusion(bf16[32,640]{1,0:T(8,128)(2,1)S(1)} %bitcast.109, bf16[512,640]{1,0:T(8,128)(2,1)S(1)} %bitcast.86, bf16[32,640]{1,0:T(8,128)(2,1)S(1)} %bitcast.106, bf16[512,640]{1,0:T(8,128)(2,1)S(1)} %bitcast.83, bf16[640,608]{0,1:T(8,128)(2,1)S(1)} %copy-done.11, bf16[640,608]{0,1:T(8,128)(2,1)S(1)} %copy-done.13), kind=kOutput, calls=%fused_computation | convolution fusion | flops 1796096000 | bytes 5734400 | tf_op jit(solution)/shard_map/dot_general | solution.py:23
  51.8 22.2 %all_to_all.20 = bf16[32,88,128]{2,1,0:T(8,128)(2,1)S(1)} all-to-all(bf16[32,88,128]{2,1,0:T(8,128)(2,1)S(1)} %maximum_maximum_fusion.1), channel_id=1, replica_groups={{0,16,32,48,64,80,96,112,128,144,160,176,192,208,224,240,256,272,288,30..., dimensions={0} | all-to-all | bytes 1441792 | tf_op jit(solution)/shard_map/all_to_all | solution.py:73
  74.0 6.7 %collective-permute-start.1 = (bf16[32,88,128]{2,1,0:T(8,128)(2,1)S(1)}, bf16[32,88,128]{2,1,0:T(8,128)(2,1)S(1)}, u32[]{:S(2)}, u32[]{:S(2)}) collective-permute-start(bf16[32,88,128]{2,1,0:T(8,128)(2,1)S(1)} %all_to_all.20), channel_id=1, source_target_pairs={{0,8},{8,0},{16,24},{24,16},{32,40},{40,32},{48,56},{56,48},{64,72... | collective-permute-start | bytes 2162696 | tf_op jit(solution)/shard_map/ppermute | solution.py:79
  80.8 1.7 collective-permute-done.1
  82.6 1.4 convolution_convert_fusion.1
  84.1 44.8 %all_to_all.21 = bf16[8,136,640]{2,1,0:T(8,128)(2,1)S(1)} all-to-all(bf16[8,136,640]{2,1,0:T(8,128)(2,1)S(1)} %bitcast.82), channel_id=1, replica_groups=mesh['expert'=64,'tensor'=8] {'tensor'}, dimensions={0} | all-to-all | bytes 2785280 | tf_op jit(solution)/shard_map/all_to_all | solution.py:115
  129.1 1.2 fusion.20
  130.4 0.8 pad_maximum_fusion.3
  131.2 24.9 %all_gather.6 = bf16[1088,480]{1,0:T(8,128)(2,1)S(1)} all-gather(bf16[136,480]{1,0:T(8,128)(2,1)S(1)} %slice.113), channel_id=1, replica_groups=mesh['expert'=64,'tensor'=8] {'tensor'}, dimensions={0}, use_global_device_ids=true | all-gather | bytes 1175040 | tf_op jit(solution)/shard_map/all_gather | solution.py:126
  156.1 24.5 %all-gather.2.cloned.1.call-done = bf16[1088,1408]{1,0:T(8,128)(2,1)} async-done(((bf16[136,1408]{1,0:T(8,128)(2,1)}), bf16[1088,1408]{1,0:T(8,128)(2,1)}) %all-gather.2.cloned.1.call-update) | async-done | bytes 3063824 | tf_op jit(solution)/shard_map/all_gather | solution.py:126
  180.6 3.0 %fusion.9 = bf16[544,640]{1,0:T(8,128)(2,1)S(1)} fusion(bf16[1088,1408]{1,0:T(8,128)(2,1)} %all-gather.2.cloned.1.call-done, bf16[640,608]{0,1:T(8,128)(2,1)} %param.12, bf16[640,608]{0,1:T(8,128)(2,1)} %param.11), kind=kOutput, calls=%fused_computation.19 | convolution fusion | flops 898191360 | bytes 3645440 | tf_op jit(solution)/shard_map/dot_general | solution.py:23
  183.6 2.8 %collective-permute-start.2 = (bf16[544,640]{1,0:T(8,128)(2,1)S(1)}, bf16[544,640]{1,0:T(8,128)(2,1)S(1)}, u32[]{:S(2)}, u32[]{:S(2)}) collective-permute-start(bf16[544,640]{1,0:T(8,128)(2,1)S(1)} %fusion.9), channel_id=1, source_target_pairs={{0,8},{8,0},{16,24},{24,16},{32,40},{40,32},{48,56},{56,48},{64,72... | collective-permute-start | bytes 2088968 | tf_op jit(solution)/shard_map/ppermute | solution.py:144
  186.5 1.3 fusion.5
  187.8 0.5 collective-permute-done.2
  188.5 1.1 maximum_maximum_fusion.2
  189.6 8.5 %all-to-all-start.3 = ((bf16[32,88,128]{2,1,0:T(8,128)(2,1)}), bf16[32,88,128]{2,1,0:T(8,128)(2,1)S(1)}, u32[]{:S(2)}, u32[]{:S(2)}) async-start(bf16[32,88,128]{2,1,0:T(8,128)(2,1)} %maximum_maximum_fusion.2), calls=%async_computation.4 | async-start | bytes 1441792 | tf_op jit(solution)/shard_map/all_to_all | solution.py:73
  198.2 1.9 convolution_convert_fusion.8
  200.1 1.1 convolution_convert_fusion.6
  201.3 0.9 pad_maximum_fusion.2
  202.2 2.3 %convolution_convert_fusion.2 = bf16[640,608]{0,1:T(8,128)(2,1)} fusion(bf16[1088,1408]{1,0:T(8,128)(2,1)S(1)} %copy-done.1, bf16[32,640]{1,0:T(8,128)(2,1)S(1)} %bitcast.110, bf16[512,640]{1,0:T(8,128)(2,1)S(1)} %bitcast.87, bf16[32,640]{1,0:T(8,128)(2,1)S(1)} %bitcast.107, bf16[512,640]{1,0:T(8,128)(2,1)S(1)} %bitcast.84), kind=kOutput, calls=%fused_computation.8 | convolution fusion | flops 852684800 | bytes 3563520 | tf_op jit(solution)/shard_map/dot_general | solution.py:23
  204.5 2.3 %convolution_convert_fusion.3 = bf16[640,608]{0,1:T(8,128)(2,1)} fusion(bf16[1088,1408]{1,0:T(8,128)(2,1)S(1)} %copy-done.1, bf16[32,640]{1,0:T(8,128)(2,1)S(1)} %bitcast.111, bf16[512,640]{1,0:T(8,128)(2,1)S(1)} %bitcast.88, bf16[32,640]{1,0:T(8,128)(2,1)S(1)} %bitcast.108, bf16[512,640]{1,0:T(8,128)(2,1)S(1)} %bitcast.85), kind=kOutput, calls=%fused_computation.9 | convolution fusion | flops 852684800 | bytes 3563520 | tf_op jit(solution)/shard_map/dot_general | solution.py:23
  206.8 8.9 %all-to-all-done.3 = bf16[32,88,128]{2,1,0:T(8,128)(2,1)S(1)} async-done(((bf16[32,88,128]{2,1,0:T(8,128)(2,1)}), bf16[32,88,128]{2,1,0:T(8,128)(2,1)S(1)}, u32[]{:S(2)}, u32[]{:S(2)}) %all-to-all-start.3) | async-done | bytes 720928 | tf_op jit(solution)/shard_map/all_to_all | solution.py:73
  215.8 1.0 convolution_convert_fusion.7
  (77 shorter events, 2.3 us)
Async XLA Ops:
  7.2 1.0 copy-start
  8.8 11.8 %copy-start.9 = (f32[128,2]{0,1:T(2,128)S(1)}, f32[128,2]{0,1:T(2,128)}, u32[]{:S(2)}) copy-start(f32[128,2]{0,1:T(2,128)} %param.10) | copy-start | bytes 3076
  8.8 36.4 %copy-start.8 = (bf16[128,640]{1,0:T(8,128)(2,1)S(1)}, bf16[128,640]{1,0:T(8,128)(2,1)}, u32[]{:S(2)}) copy-start(bf16[128,640]{1,0:T(8,128)(2,1)} %param.8) | copy-start | bytes 491524
  10.0 28.9 %all-to-all-start = ((bf16[32,88,128]{2,1,0:T(8,128)(2,1)}), bf16[32,88,128]{2,1,0:T(8,128)(2,1)S(1)}, u32[]{:S(2)}, u32[]{:S(2)}) async-start(bf16[32,88,128]{2,1,0:T(8,128)(2,1)} %maximum_maximum_fusion), calls=%async_computation | async-start | bytes 1441792 | tf_op jit(solution)/shard_map/all_to_all | solution.py:73
  20.5 108.6 %reduce-scatter.2.cloned.1.call-start = ((), (), s32[]{:S(2)}) async-start(), calls=%async_computation.5 | async-start | bytes 3133440 | tf_op jit(solution)/shard_map/reduce_scatter | solution.py:109
  38.9 8.1 %collective-permute-start = (bf16[32,88,128]{2,1,0:T(8,128)(2,1)S(1)}, bf16[32,88,128]{2,1,0:T(8,128)(2,1)S(1)}, u32[]{:S(2)}, u32[]{:S(2)}) collective-permute-start(bf16[32,88,128]{2,1,0:T(8,128)(2,1)S(1)} %all-to-all-done), channel_id=1, source_target_pairs={{0,8},{8,0},{16,24},{24,16},{32,40},{40,32},{48,56},{56,48},{64,72... | collective-permute-start | bytes 2162696 | tf_op jit(solution)/shard_map/ppermute | solution.py:79
  46.2 1.6 copy-start.11
  46.2 1.6 copy-start.13
  47.0 0.8 copy-start.2
  51.8 128.8 %all-gather.2.cloned.1.call-start = ((), (), s32[]{:S(2)}) async-start(), calls=%async_computation.6 | async-start | bytes 3446784 | tf_op jit(solution)/shard_map/all_gather | solution.py:126
  74.0 8.6 %copy-start.10 = (bf16[608,640]{1,0:T(8,128)(2,1)S(1)}, bf16[608,640]{1,0:T(8,128)(2,1)}, u32[]{:S(2)}) copy-start(bf16[608,640]{1,0:T(8,128)(2,1)} %param.13) | copy-start | bytes 2334724
  74.0 8.5 %collective-permute-start.1 = (bf16[32,88,128]{2,1,0:T(8,128)(2,1)S(1)}, bf16[32,88,128]{2,1,0:T(8,128)(2,1)S(1)}, u32[]{:S(2)}, u32[]{:S(2)}) collective-permute-start(bf16[32,88,128]{2,1,0:T(8,128)(2,1)S(1)} %all_to_all.20), channel_id=1, source_target_pairs={{0,8},{8,0},{16,24},{24,16},{32,40},{40,32},{48,56},{56,48},{64,72... | collective-permute-start | bytes 2162696 | tf_op jit(solution)/shard_map/ppermute | solution.py:79
  80.8 3.2 %copy-start.4 = (bf16[32,80,128]{2,1,0:T(8,128)(2,1)}, bf16[32,80,128]{2,1,0:T(8,128)(2,1)S(1)}, u32[]{:S(2)}) copy-start(bf16[32,80,128]{2,1,0:T(8,128)(2,1)S(1)} %slice.114) | copy-start | bytes 1966084
  82.6 1.4 copy-start.6
  183.6 2.9 %slice-start = ((bf16[1088,1408]{1,0:T(8,128)(2,1)}), bf16[1088,1280]{1,0:T(8,128)(2,1)S(1)}, s32[]{:S(2)}) async-start(bf16[1088,1408]{1,0:T(8,128)(2,1)} %all-gather.2.cloned.1.call-done), calls=%async_computation.7 | async-start | bytes 5570560 | tf_op jit(solution)/shard_map/slice | solution.py:134
  183.6 2.9 %copy-start.12 = (bf16[640,608]{0,1:T(8,128)(2,1)S(1)}, bf16[640,608]{0,1:T(8,128)(2,1)}, u32[]{:S(2)}) copy-start(bf16[640,608]{0,1:T(8,128)(2,1)} %param.12) | copy-start | bytes 2334724
  183.6 2.9 %copy-start.14 = (bf16[640,608]{0,1:T(8,128)(2,1)S(1)}, bf16[640,608]{0,1:T(8,128)(2,1)}, u32[]{:S(2)}) copy-start(bf16[640,608]{0,1:T(8,128)(2,1)} %param.11) | copy-start | bytes 2334724
  183.6 4.6 %collective-permute-start.2 = (bf16[544,640]{1,0:T(8,128)(2,1)S(1)}, bf16[544,640]{1,0:T(8,128)(2,1)S(1)}, u32[]{:S(2)}, u32[]{:S(2)}) collective-permute-start(bf16[544,640]{1,0:T(8,128)(2,1)S(1)} %fusion.9), channel_id=1, source_target_pairs={{0,8},{8,0},{16,24},{24,16},{32,40},{40,32},{48,56},{56,48},{64,72... | collective-permute-start | bytes 2088968 | tf_op jit(solution)/shard_map/ppermute | solution.py:144
  189.6 26.1 %all-to-all-start.3 = ((bf16[32,88,128]{2,1,0:T(8,128)(2,1)}), bf16[32,88,128]{2,1,0:T(8,128)(2,1)S(1)}, u32[]{:S(2)}, u32[]{:S(2)}) async-start(bf16[32,88,128]{2,1,0:T(8,128)(2,1)} %maximum_maximum_fusion.2), calls=%async_computation.4 | async-start | bytes 1441792 | tf_op jit(solution)/shard_map/all_to_all | solution.py:73
  198.2 2.0 copy-start.5
  198.2 2.0 copy-start.7
  200.1 2.1 copy-start.1
  200.1 2.1 copy-start.3
Sparse Core Ops, SparseCore 0:
  51.9 43.9 reduce-scatter.1
  131.3 49.1 all-gather.1

commit v4 on v3

--- a/solution.py
+++ b/solution.py
@@ -74,11 +74,11 @@
             rows, "expert", split_axis=0, concat_axis=0, tiled=True, axis_index_groups=same_core
         )
 
-    def routed(send):
-        mine = exchange(send)
-        theirs = lax.ppermute(mine, "expert", other_core)
-        (main_a, last_a), (main_b, last_b) = unfold(mine), unfold(theirs)
-        return jnp.concatenate([main_a, last_a, main_b, last_b], axis=0)
+    def swapped(array):
+        return lax.ppermute(array, "expert", other_core)
+
+    def received(send):
+        return jnp.concatenate(unfold(exchange(send)), axis=0)
 
     main = chips * MAIN
     half = main + chips
@@ -98,20 +98,27 @@
             for pair in zip(chosen(first), chosen(second), strict=True)
         )
     )
-    local_x = routed(send_x)
 
     hidden_units = w_gate.shape[1]
     width = -(-hidden_units // LANES) * LANES
     pad = ((0, 0), (0, width - hidden_units))
     w_both = jnp.concatenate([jnp.pad(w_gate, pad), jnp.pad(w_up, pad)], axis=1)
-    parts = matmul(local_x, w_both).astype(bf16)
+    w_back = jnp.pad(w_down, pad[::-1])
+    w_both_other, w_back_other = swapped(w_both), swapped(w_back)
+
+    local_x = received(send_x)
+    parts = jnp.concatenate(
+        [matmul(local_x, w).astype(bf16) for w in (w_both, w_both_other)], axis=0
+    )
     parts, send_grad = lax.optimization_barrier((parts, send_grad))
     sums = lax.psum_scatter(parts, "tensor", scatter_dimension=0, tiled=True)
     gate, up = (sums[:, k * width : (k + 1) * width].astype(jnp.float32) for k in range(2))
 
-    local_grad = routed(send_grad)
+    local_grad = received(send_grad)
     shards = lax.axis_size("tensor")
-    pieces = matmul(local_grad, jnp.pad(w_down, pad[::-1]), 1, 1).astype(bf16)
+    pieces = jnp.concatenate(
+        [matmul(local_grad, w, 1, 1).astype(bf16) for w in (w_back, w_back_other)], axis=0
+    )
     pieces = lax.all_to_all(
         pieces.reshape(shards, pieces.shape[0] // shards, width),
         "tensor",
@@ -130,20 +137,33 @@
     acts = spread(
         jnp.concatenate([grad_act_gate, grad_act_up, hidden[:, cut:hidden_units]], axis=1)
     )
-    most, acts = lax.optimization_barrier((most, acts))
-    acts, least = acts[:, : 2 * width], acts[:, 2 * width :]
-    grad_down = jnp.concatenate(
-        [matmul(part, local_grad, 0, 0).astype(bf16) for part in (most, least)], axis=0
+
+    most, local_x, local_grad = lax.optimization_barrier((most, local_x, local_grad))
+
+    def both_cores(own, other):
+        return jnp.concatenate([own, other], axis=0)
+
+    all_x = both_cores(local_x, swapped(local_x))
+    all_grad = both_cores(local_grad, swapped(local_grad))
+    all_most = both_cores(most[:half], swapped(most[half:]))
+    down = matmul(all_most, all_grad, 0, 0).astype(bf16)
+    down, all_x, all_grad, acts = lax.optimization_barrier((down, all_x, all_grad, acts))
+
+    rows = matmul(acts[:half, : 2 * width], w_both, 1, 1)
+    rows = rows + matmul(acts[half:, : 2 * width], w_both_other, 1, 1)
+    rows = rows.astype(bf16)
+    send_back = fold(rows[:main], rows[main:])
+    send_back, acts = lax.optimization_barrier((send_back, acts))
+    returned = exchange(send_back)
+    all_acts = both_cores(acts[:half], swapped(acts)[half:])
+    grad_gate = matmul(all_x, all_acts[:, :hidden_units], 0, 0).astype(bf16)
+    grad_up = matmul(all_x, all_acts[:, width : width + hidden_units], 0, 0).astype(bf16)
+    least = matmul(all_acts[:, 2 * width :], all_grad, 0, 0).astype(bf16)
+    grad_down = jnp.concatenate([down, least], axis=0)
+    returned, grad_gate, grad_up, grad_down = lax.optimization_barrier(
+        (returned, grad_gate, grad_up, grad_down)
     )
-    grad_gate = matmul(local_x, acts[:, :hidden_units], 0, 0).astype(bf16)
-    grad_up = matmul(local_x, acts[:, width : width + hidden_units], 0, 0).astype(bf16)
-
-    away = matmul(acts[half:], w_both, 1, 1).astype(bf16)
-    away, acts = lax.optimization_barrier((away, acts))
-    here = lax.optimization_barrier(matmul(acts[:half], w_both, 1, 1))
-    away = lax.ppermute(away, "expert", other_core)
-    chip_rows = (here + away.astype(jnp.float32)).astype(bf16)
-    returned = jnp.concatenate(unfold(exchange(fold(chip_rows[:main], chip_rows[main:]))), axis=0)
+    returned = jnp.concatenate(unfold(returned), axis=0)
     taking = jnp.concatenate(chosen(named), axis=0)
     grad_tokens = matmul(taking, returned, 0, 0).astype(bf16)
     return (grad_tokens, grad_gate, grad_up, grad_down)

time: 228 us -> 226 us (level)
  blocking collectives: 91.9 us -> 71.8 us
  starting transfers between devices: 34.9 us -> 51.1 us
  waiting for transfers between devices: 54.5 us -> 43.3 us
  other arithmetic: 5.78 us -> 11.3 us
  local copies, waits for them, and re-layouts: 2.56 us -> 7.3 us
  matrix products: 19.4 us -> 22.9 us
    all_to_all x1 -> x0, blocking collectives: 22.2 us -> none  [exchange(): lax.all_to_all(rows, 'expert', split_axis=0, concat_axis=0, tiled=True, a...]
    all_gather x1, waiting for transfers between devices: 24.5 us -> 9.54 us  [spread(): return lax.all_gather(part, 'tensor', axis=0, tiled=True)]
    all_to_all x2 -> x3, starting transfers between devices: 19 us -> 28.3 us  [exchange(): lax.all_to_all(rows, 'expert', split_axis=0, concat_axis=0, tiled=True, a...]
    ppermute x3 -> x6, starting transfers between devices: 15.8 us -> 22.7 us  [swapped(): return lax.ppermute(array, 'expert', other_core)]
    all_to_all x2 -> x3, waiting for transfers between devices: 27.2 us -> 33.7 us  [exchange(): lax.all_to_all(rows, 'expert', split_axis=0, concat_axis=0, tiled=True, a...]
    concatenate x1 -> x7, other arithmetic: 0.95 us -> 5.66 us  [the longest x1 1.73 us: on_device(): jnp.concatenate([matmul(local_x, w).astype(bf16) for w in (w_both, w_both...]
    dot_general x14 -> x16, matrix products: 19.4 us -> 22.9 us  [matmul(): lax.dot_general(a, b, (((a_dim,), (b_dim,)), ((), ())), preferred_element...]
    slice x4 -> x5, local copies, waits for them, and re-layouts: 0.07 us -> 3.15 us  [the longest x2 3.02 us: on_device(): all_acts = both_cores(acts[:half], swapped(acts)[half:])]
  transfers between devices with their start and end apart: 7 -> 11, of which waited for: 6 -> 4; matrix products, arithmetic and copies ran while one was open for 6% -> 11% of each run, Pallas kernels for 0% -> 0%
where the time goes in v4:
time: 226 us; the launch traced here: 222 us
  blocking collectives  71.8 us (32%)
  starting transfers between devices  51.1 us (23%)
  waiting for transfers between devices  43.3 us (19%)
  matrix products  22.9 us (10%)
  between operations  14.5 us (6%)
  other arithmetic  11.3 us (5%)
  local copies, waits for them, and re-layouts  7.3 us (3%)
    all_to_all x1, blocking collectives, on_device(): lax.all_to_all(pieces.reshape(shards, pieces.shape[0] // shards, width),...  46.5 us
    all_to_all x3, waiting for transfers between devices, exchange(): lax.all_to_all(rows, 'expert', split_axis=0, concat_axis=0, tiled=True, a...  33.7 us
    all_to_all x3, starting transfers between devices, exchange(): lax.all_to_all(rows, 'expert', split_axis=0, concat_axis=0, tiled=True, a...  28.3 us
    all_gather x1, blocking collectives, spread(): return lax.all_gather(part, 'tensor', axis=0, tiled=True)  25.3 us
    dot_general x16, matrix products, matmul(): lax.dot_general(a, b, (((a_dim,), (b_dim,)), ((), ())), preferred_element...  22.9 us
    ppermute x6, starting transfers between devices, swapped(): return lax.ppermute(array, 'expert', other_core)  22.7 us
    all_gather x1, waiting for transfers between devices, spread(): return lax.all_gather(part, 'tensor', axis=0, tiled=True)  9.54 us
  transfers between devices with their start and end apart: 11, of which 4 were waited for; matrix products, arithmetic and copies ran while one was open for 11% of the time, Pallas kernels for 0%

profile of v4, /device:TPU:1, one launch (start us, length us, event | category | flops | bytes accessed | tf_op | source)
XLA Modules:
  0.0 222.3 jit_solution(16882841550970720130)
XLA Ops:
  9.9 10.5 %all-to-all-start = ((bf16[32,88,128]{2,1,0:T(8,128)(2,1)}), bf16[32,88,128]{2,1,0:T(8,128)(2,1)S(1)}, u32[]{:S(2)}, u32[]{:S(2)}) async-start(bf16[32,88,128]{2,1,0:T(8,128)(2,1)} %maximum_maximum_fusion), calls=%async_computation | async-start | bytes 1441792 | tf_op jit(solution)/shard_map/all_to_all | solution.py:73
  20.5 1.5 fusion.2
  22.0 2.9 %collective-permute-start = (bf16[640,1280]{0,1:T(8,128)(2,1)S(1)}, bf16[640,1280]{0,1:T(8,128)(2,1)}, u32[]{:S(2)}, u32[]{:S(2)}) collective-permute-start(bf16[640,1280]{0,1:T(8,128)(2,1)S(1)} %fusion.2), channel_id=1, source_target_pairs={{0,8},{8,0},{16,24},{24,16},{32,40},{40,32},{48,56},{56,48},{64,72... | collective-permute-start | bytes 4915208 | tf_op jit(solution)/shard_map/ppermute | solution.py:78
  26.9 11.9 %all-to-all-done = bf16[32,88,128]{2,1,0:T(8,128)(2,1)S(1)} async-done(((bf16[32,88,128]{2,1,0:T(8,128)(2,1)}), bf16[32,88,128]{2,1,0:T(8,128)(2,1)S(1)}, u32[]{:S(2)}, u32[]{:S(2)}) %all-to-all-start) | async-done | bytes 720928 | tf_op jit(solution)/shard_map/all_to_all | solution.py:73
  38.9 2.6 %convolution_convert_fusion.1 = bf16[544,1280]{1,0:T(8,128)(2,1)S(1)} fusion(bf16[32,640]{1,0:T(8,128)(2,1)S(1)} %bitcast.84, bf16[512,640]{1,0:T(8,128)(2,1)S(1)} %bitcast.69, bf16[640,608]{0,1:T(8,128)(2,1)} %param.12, bf16[640,608]{0,1:T(8,128)(2,1)} %param.11), kind=kOutput, calls=%fused_computation.9 | convolution fusion | flops 899932160 | bytes 3645440 | tf_op jit(solution)/shard_map/dot_general | solution.py:23
  41.6 2.7 %convolution_convert_fusion = bf16[544,1280]{1,0:T(8,128)(2,1)S(1)} fusion(bf16[640,1280]{0,1:T(8,128)(2,1)} %collective-permute-done, bf16[32,640]{1,0:T(8,128)(2,1)S(1)} %bitcast.85, bf16[512,640]{1,0:T(8,128)(2,1)S(1)} %bitcast.70), kind=kOutput, calls=%fused_computation.8 | convolution fusion | flops 893378560 | bytes 3727360 | tf_op jit(solution)/shard_map/dot_general | solution.py:23
  44.3 1.7 pad_maximum_fusion
  46.0 7.8 %all-to-all-start.1 = ((bf16[32,88,128]{2,1,0:T(8,128)(2,1)}), bf16[32,88,128]{2,1,0:T(8,128)(2,1)S(1)}, u32[]{:S(2)}, u32[]{:S(2)}) async-start(bf16[32,88,128]{2,1,0:T(8,128)(2,1)} %maximum_maximum_fusion.1), calls=%async_computation.2 | async-start | bytes 1441792 | tf_op jit(solution)/shard_map/all_to_all | solution.py:73
  53.9 1.2 pad.13
  55.1 3.3 %collective-permute-start.4 = (bf16[640,640]{1,0:T(8,128)(2,1)S(1)}, bf16[640,640]{1,0:T(8,128)(2,1)}, u32[]{:S(2)}, u32[]{:S(2)}) collective-permute-start(bf16[640,640]{1,0:T(8,128)(2,1)S(1)} %pad.13), channel_id=1, source_target_pairs={{0,8},{8,0},{16,24},{24,16},{32,40},{40,32},{48,56},{56,48},{64,72... | collective-permute-start | bytes 2457608 | tf_op jit(solution)/shard_map/ppermute | solution.py:78
  58.5 13.3 %all-to-all-done.1 = bf16[32,88,128]{2,1,0:T(8,128)(2,1)S(1)} async-done(((bf16[32,88,128]{2,1,0:T(8,128)(2,1)}), bf16[32,88,128]{2,1,0:T(8,128)(2,1)S(1)}, u32[]{:S(2)}, u32[]{:S(2)}) %all-to-all-start.1) | async-done | bytes 720928 | tf_op jit(solution)/shard_map/all_to_all | solution.py:73
  71.8 1.9 convolution_convert_fusion.5
  73.8 2.0 convolution_convert_fusion.4
  75.8 46.5 %all_to_all.20 = bf16[8,136,640]{2,1,0:T(8,128)(2,1)S(1)} all-to-all(bf16[8,136,640]{2,1,0:T(8,128)(2,1)S(1)} %bitcast.68), channel_id=1, replica_groups=mesh['expert'=64,'tensor'=8] {'tensor'}, dimensions={0} | all-to-all | bytes 2785280 | tf_op jit(solution)/shard_map/all_to_all | solution.py:122
  122.6 1.2 fusion.23
  124.9 25.3 %all_gather.6 = bf16[1088,480]{1,0:T(8,128)(2,1)S(1)} all-gather(bf16[136,480]{1,0:T(8,128)(2,1)S(1)} %slice.104), channel_id=1, replica_groups=mesh['expert'=64,'tensor'=8] {'tensor'}, dimensions={0}, use_global_device_ids=true | all-gather | bytes 1175040 | tf_op jit(solution)/shard_map/all_gather | solution.py:133
  150.1 9.8 %collective-permute-start.2 = (bf16[544,640]{1,0:T(8,128)(2,1)S(1)}, bf16[544,640]{1,0:T(8,128)(2,1)S(1)}, u32[]{:S(2)}, u32[]{:S(2)}) collective-permute-start(bf16[544,640]{1,0:T(8,128)(2,1)S(1)} %pad_maximum_fusion.5), channel_id=1, source_target_pairs={{0,8},{8,0},{16,24},{24,16},{32,40},{40,32},{48,56},{56,48},{64,72... | collective-permute-start | bytes 2088968 | tf_op jit(solution)/shard_map/ppermute | solution.py:78
  160.1 1.9 collective-permute-start.1
  162.0 2.4 %collective-permute-start.3 = (bf16[544,640]{1,0:T(8,128)(2,1)S(1)}, bf16[544,640]{1,0:T(8,128)(2,1)S(1)}, u32[]{:S(2)}, u32[]{:S(2)}) collective-permute-start(bf16[544,640]{1,0:T(8,128)(2,1)S(1)} %pad_maximum_fusion.4), channel_id=1, source_target_pairs={{0,8},{8,0},{16,24},{24,16},{32,40},{40,32},{48,56},{56,48},{64,72... | collective-permute-start | bytes 2088968 | tf_op jit(solution)/shard_map/ppermute | solution.py:78
  164.6 1.9 convolution_convert_fusion.8
  166.5 1.2 pad_maximum_fusion.1
  167.8 9.5 %all-gather.2.cloned.1.call-done = bf16[1088,1408]{1,0:T(8,128)(2,1)} async-done(((bf16[136,1408]{1,0:T(8,128)(2,1)}), bf16[1088,1408]{1,0:T(8,128)(2,1)}) %all-gather.2.cloned.1.call-update) | async-done | bytes 3063824 | tf_op jit(solution)/shard_map/all_gather | solution.py:133
  177.3 3.2 %fusion.7 = f32[544,640]{1,0:T(8,128)S(1)} fusion(bf16[640,1280]{0,1:T(8,128)(2,1)} %collective-permute-done, bf16[1088,1408]{1,0:T(8,128)(2,1)} %all-gather.2.cloned.1.call-done), kind=kOutput, calls=%fused_computation.20 | convolution fusion | flops 891289600 | bytes 4423680 | tf_op jit(solution)/shard_map/dot_general | solution.py:23
  180.6 1.3 add_convert_fusion
  182.0 1.1 maximum_maximum_fusion.2
  183.1 2.4 %collective-permute-start.5 = (bf16[1088,1408]{1,0:T(8,128)(2,1)}, bf16[1088,1408]{1,0:T(8,128)(2,1)}, u32[]{:S(2)}, u32[]{:S(2)}) collective-permute-start(bf16[1088,1408]{1,0:T(8,128)(2,1)} %all-gather.2.cloned.1.call-done), channel_id=1, source_target_pairs={{0,8},{8,0},{16,24},{24,16},{32,40},{40,32},{48,56},{56,48},{64,72... | collective-permute-start | bytes 9191432 | tf_op jit(solution)/shard_map/ppermute | solution.py:78
  185.5 10.0 %all-to-all-start.3 = ((bf16[32,88,128]{2,1,0:T(8,128)(2,1)}), bf16[32,88,128]{2,1,0:T(8,128)(2,1)S(1)}, u32[]{:S(2)}, u32[]{:S(2)}) async-start(bf16[32,88,128]{2,1,0:T(8,128)(2,1)} %maximum_maximum_fusion.2), calls=%async_computation.4 | async-start | bytes 1441792 | tf_op jit(solution)/shard_map/all_to_all | solution.py:73
  195.5 1.5 slice.93
  197.1 1.5 slice.110
  201.3 2.3 %convolution_convert_fusion.2 = bf16[640,608]{0,1:T(8,128)(2,1)} fusion(bf16[1088,640]{1,0:T(8,128)(2,1)S(1)} %copy-done.1, bf16[544,1408]{1,0:T(8,128)(2,1)S(1)} %slice.93, bf16[544,1408]{1,0:T(8,128)(2,1)S(1)} %slice.110), kind=kOutput, calls=%fused_computation.13 | convolution fusion | flops 849760256 | bytes 5234688 | tf_op jit(solution)/shard_map/dot_general | solution.py:23
  203.6 2.3 %convolution_convert_fusion.3 = bf16[640,608]{0,1:T(8,128)(2,1)} fusion(bf16[1088,640]{1,0:T(8,128)(2,1)S(1)} %copy-done.1, bf16[544,1408]{1,0:T(8,128)(2,1)S(1)} %slice.93, bf16[544,1408]{1,0:T(8,128)(2,1)S(1)} %slice.110), kind=kOutput, calls=%fused_computation.14 | convolution fusion | flops 849760256 | bytes 5234688 | tf_op jit(solution)/shard_map/dot_general | solution.py:23
  205.9 8.5 %all-to-all-done.3 = bf16[32,88,128]{2,1,0:T(8,128)(2,1)S(1)} async-done(((bf16[32,88,128]{2,1,0:T(8,128)(2,1)}), bf16[32,88,128]{2,1,0:T(8,128)(2,1)S(1)}, u32[]{:S(2)}, u32[]{:S(2)}) %all-to-all-start.3) | async-done | bytes 720928 | tf_op jit(solution)/shard_map/all_to_all | solution.py:73
  (75 shorter events, 10.3 us)
Async XLA Ops:
  7.2 1.0 copy-start
  9.9 28.9 %all-to-all-start = ((bf16[32,88,128]{2,1,0:T(8,128)(2,1)}), bf16[32,88,128]{2,1,0:T(8,128)(2,1)S(1)}, u32[]{:S(2)}, u32[]{:S(2)}) async-start(bf16[32,88,128]{2,1,0:T(8,128)(2,1)} %maximum_maximum_fusion), calls=%async_computation | async-start | bytes 1441792 | tf_op jit(solution)/shard_map/all_to_all | solution.py:73
  20.4 4.5 %copy-start.7 = (f32[128,2]{0,1:T(2,128)S(1)}, f32[128,2]{0,1:T(2,128)}, u32[]{:S(2)}) copy-start(f32[128,2]{0,1:T(2,128)} %param.10) | copy-start | bytes 3076
  20.4 4.5 %copy-start.6 = (bf16[128,640]{1,0:T(8,128)(2,1)S(1)}, bf16[128,640]{1,0:T(8,128)(2,1)}, u32[]{:S(2)}) copy-start(bf16[128,640]{1,0:T(8,128)(2,1)} %param.8) | copy-start | bytes 491524
  20.5 102.1 %reduce-scatter.2.cloned.1.call-start = ((), (), s32[]{:S(2)}) async-start(), calls=%async_computation.5 | async-start | bytes 3133440 | tf_op jit(solution)/shard_map/reduce_scatter | solution.py:114
  22.0 19.5 %collective-permute-start = (bf16[640,1280]{0,1:T(8,128)(2,1)S(1)}, bf16[640,1280]{0,1:T(8,128)(2,1)}, u32[]{:S(2)}, u32[]{:S(2)}) collective-permute-start(bf16[640,1280]{0,1:T(8,128)(2,1)S(1)} %fusion.2), channel_id=1, source_target_pairs={{0,8},{8,0},{16,24},{24,16},{32,40},{40,32},{48,56},{56,48},{64,72... | collective-permute-start | bytes 4915208 | tf_op jit(solution)/shard_map/ppermute | solution.py:78
  46.0 25.7 %all-to-all-start.1 = ((bf16[32,88,128]{2,1,0:T(8,128)(2,1)}), bf16[32,88,128]{2,1,0:T(8,128)(2,1)S(1)}, u32[]{:S(2)}, u32[]{:S(2)}) async-start(bf16[32,88,128]{2,1,0:T(8,128)(2,1)} %maximum_maximum_fusion.1), calls=%async_computation.2 | async-start | bytes 1441792 | tf_op jit(solution)/shard_map/all_to_all | solution.py:73
  53.9 123.4 %all-gather.2.cloned.1.call-start = ((), (), s32[]{:S(2)}) async-start(), calls=%async_computation.6 | async-start | bytes 3446784 | tf_op jit(solution)/shard_map/all_gather | solution.py:133
  55.1 18.6 %collective-permute-start.4 = (bf16[640,640]{1,0:T(8,128)(2,1)S(1)}, bf16[640,640]{1,0:T(8,128)(2,1)}, u32[]{:S(2)}, u32[]{:S(2)}) collective-permute-start(bf16[640,640]{1,0:T(8,128)(2,1)S(1)} %pad.13), channel_id=1, source_target_pairs={{0,8},{8,0},{16,24},{24,16},{32,40},{40,32},{48,56},{56,48},{64,72... | collective-permute-start | bytes 2457608 | tf_op jit(solution)/shard_map/ppermute | solution.py:78
  150.1 14.3 %collective-permute-start.2 = (bf16[544,640]{1,0:T(8,128)(2,1)S(1)}, bf16[544,640]{1,0:T(8,128)(2,1)S(1)}, u32[]{:S(2)}, u32[]{:S(2)}) collective-permute-start(bf16[544,640]{1,0:T(8,128)(2,1)S(1)} %pad_maximum_fusion.5), channel_id=1, source_target_pairs={{0,8},{8,0},{16,24},{24,16},{32,40},{40,32},{48,56},{56,48},{64,72... | collective-permute-start | bytes 2088968 | tf_op jit(solution)/shard_map/ppermute | solution.py:78
  160.1 4.5 %collective-permute-start.1 = (bf16[544,480]{1,0:T(8,128)(2,1)S(1)}, bf16[544,480]{1,0:T(8,128)(2,1)S(1)}, u32[]{:S(2)}, u32[]{:S(2)}) collective-permute-start(bf16[544,480]{1,0:T(8,128)(2,1)S(1)} %get-tuple-element.47), channel_id=1, source_target_pairs={{0,8},{8,0},{16,24},{24,16},{32,40},{40,32},{48,56},{56,48},{64,72... | collective-permute-start | bytes 1566728 | tf_op jit(solution)/shard_map/ppermute | solution.py:78
  162.0 4.6 %collective-permute-start.3 = (bf16[544,640]{1,0:T(8,128)(2,1)S(1)}, bf16[544,640]{1,0:T(8,128)(2,1)S(1)}, u32[]{:S(2)}, u32[]{:S(2)}) collective-permute-start(bf16[544,640]{1,0:T(8,128)(2,1)S(1)} %pad_maximum_fusion.4), channel_id=1, source_target_pairs={{0,8},{8,0},{16,24},{24,16},{32,40},{40,32},{48,56},{56,48},{64,72... | collective-permute-start | bytes 2088968 | tf_op jit(solution)/shard_map/ppermute | solution.py:78
  167.8 12.8 %copy-start.2 = (bf16[640,608]{0,1:T(8,128)(2,1)S(1)}, bf16[640,608]{0,1:T(8,128)(2,1)}, u32[]{:S(2)}) copy-start(bf16[640,608]{0,1:T(8,128)(2,1)} %param.12) | copy-start | bytes 2334724
  167.8 12.8 %copy-start.3 = (bf16[640,608]{0,1:T(8,128)(2,1)S(1)}, bf16[640,608]{0,1:T(8,128)(2,1)}, u32[]{:S(2)}) copy-start(bf16[640,608]{0,1:T(8,128)(2,1)} %param.11) | copy-start | bytes 2334724
  177.3 3.3 %copy-start.4 = (bf16[1088,1408]{1,0:T(8,128)(2,1)S(1)}, bf16[1088,1408]{1,0:T(8,128)(2,1)}, u32[]{:S(2)}) copy-start(bf16[1088,1408]{1,0:T(8,128)(2,1)} %all-gather.2.cloned.1.call-done) | copy-start | bytes 9191428
  183.1 13.9 %collective-permute-start.5 = (bf16[1088,1408]{1,0:T(8,128)(2,1)}, bf16[1088,1408]{1,0:T(8,128)(2,1)}, u32[]{:S(2)}, u32[]{:S(2)}) collective-permute-start(bf16[1088,1408]{1,0:T(8,128)(2,1)} %all-gather.2.cloned.1.call-done), channel_id=1, source_target_pairs={{0,8},{8,0},{16,24},{24,16},{32,40},{40,32},{48,56},{56,48},{64,72... | collective-permute-start | bytes 9191432 | tf_op jit(solution)/shard_map/ppermute | solution.py:78
  185.5 28.8 %all-to-all-start.3 = ((bf16[32,88,128]{2,1,0:T(8,128)(2,1)}), bf16[32,88,128]{2,1,0:T(8,128)(2,1)S(1)}, u32[]{:S(2)}, u32[]{:S(2)}) async-start(bf16[32,88,128]{2,1,0:T(8,128)(2,1)} %maximum_maximum_fusion.2), calls=%async_computation.4 | async-start | bytes 1441792 | tf_op jit(solution)/shard_map/all_to_all | solution.py:73
  198.6 1.1 copy-start.5
  199.7 1.6 copy-start.1
Sparse Core Ops, SparseCore 0:
  46.2 53.3 reduce-scatter.1
  124.8 52.4 all-gather.1

commit v5 on v4

--- a/solution.py
+++ b/solution.py
@@ -116,9 +116,13 @@
 
     local_grad = received(send_grad)
     shards = lax.axis_size("tensor")
-    pieces = jnp.concatenate(
-        [matmul(local_grad, w, 1, 1).astype(bf16) for w in (w_back, w_back_other)], axis=0
+    pieces = lax.dot_general(
+        jnp.broadcast_to(local_grad, (CORES, *local_grad.shape)),
+        jnp.stack([w_back, w_back_other]),
+        (((2,), (2,)), ((0,), (0,))),
+        preferred_element_type=jnp.float32,
     )
+    pieces = pieces.astype(bf16).reshape(CORES * half, width)
     pieces = lax.all_to_all(
         pieces.reshape(shards, pieces.shape[0] // shards, width),
         "tensor",

time: 226 us -> 226 us (level)
    dot_general x16 -> x14, matrix products: 22.9 us -> 18.2 us  [matmul(): lax.dot_general(a, b, (((a_dim,), (b_dim,)), ((), ())), preferred_element...]
    dot_general x0 -> x1, matrix products: none -> 2.59 us  [on_device(): lax.dot_general(jnp.broadcast_to(local_grad, (CORES, *local_grad.shape)),...]
  transfers between devices with their start and end apart: 11 -> 11, of which waited for: 4 -> 5; matrix products, arithmetic and copies ran while one was open for 11% -> 10% of each run, Pallas kernels for 0% -> 0%
where the time goes in v5:
time: 226 us; the launch traced here: 222 us
  blocking collectives  72.6 us (32%)
  starting transfers between devices  51.8 us (23%)
  waiting for transfers between devices  43.8 us (19%)
  matrix products  20.8 us (9%)
  between operations  14.6 us (6%)
  other arithmetic  11.2 us (5%)
  local copies, waits for them, and re-layouts  7.68 us (3%)
    all_to_all x1, blocking collectives, on_device(): lax.all_to_all(pieces.reshape(shards, pieces.shape[0] // shards, width),...  47.9 us
    all_to_all x3, waiting for transfers between devices, exchange(): lax.all_to_all(rows, 'expert', split_axis=0, concat_axis=0, tiled=True, a...  33.1 us
    all_to_all x3, starting transfers between devices, exchange(): lax.all_to_all(rows, 'expert', split_axis=0, concat_axis=0, tiled=True, a...  28.6 us
    all_gather x1, blocking collectives, spread(): return lax.all_gather(part, 'tensor', axis=0, tiled=True)  24.6 us
    ppermute x6, starting transfers between devices, swapped(): return lax.ppermute(array, 'expert', other_core)  23.1 us
    dot_general x14, matrix products, matmul(): lax.dot_general(a, b, (((a_dim,), (b_dim,)), ((), ())), preferred_element...  18.2 us
    all_gather x1, waiting for transfers between devices, spread(): return lax.all_gather(part, 'tensor', axis=0, tiled=True)  10.1 us
  transfers between devices with their start and end apart: 11, of which 5 were waited for; matrix products, arithmetic and copies ran while one was open for 10% of the time, Pallas kernels for 0%

profile of v5, /device:TPU:1, one launch (start us, length us, event | category | flops | bytes accessed | tf_op | source)
XLA Modules:
  0.0 222.3 jit_solution(14265883862473830326)
XLA Ops:
  8.9 1.1 maximum_maximum_fusion
  9.9 10.5 %all-to-all-start = ((bf16[32,88,128]{2,1,0:T(8,128)(2,1)}), bf16[32,88,128]{2,1,0:T(8,128)(2,1)S(1)}, u32[]{:S(2)}, u32[]{:S(2)}) async-start(bf16[32,88,128]{2,1,0:T(8,128)(2,1)} %maximum_maximum_fusion), calls=%async_computation | async-start | bytes 1441792 | tf_op jit(solution)/shard_map/all_to_all | solution.py:73
  20.5 1.5 fusion.2
  22.1 2.9 %collective-permute-start = (bf16[640,1280]{0,1:T(8,128)(2,1)S(1)}, bf16[640,1280]{0,1:T(8,128)(2,1)}, u32[]{:S(2)}, u32[]{:S(2)}) collective-permute-start(bf16[640,1280]{0,1:T(8,128)(2,1)S(1)} %fusion.2), channel_id=1, source_target_pairs={{0,8},{8,0},{16,24},{24,16},{32,40},{40,32},{48,56},{56,48},{64,72... | collective-permute-start | bytes 4915208 | tf_op jit(solution)/shard_map/ppermute | solution.py:78
  26.9 11.9 %all-to-all-done = bf16[32,88,128]{2,1,0:T(8,128)(2,1)S(1)} async-done(((bf16[32,88,128]{2,1,0:T(8,128)(2,1)}), bf16[32,88,128]{2,1,0:T(8,128)(2,1)S(1)}, u32[]{:S(2)}, u32[]{:S(2)}) %all-to-all-start) | async-done | bytes 720928 | tf_op jit(solution)/shard_map/all_to_all | solution.py:73
  38.9 2.6 %convolution_convert_fusion.1 = bf16[544,1280]{1,0:T(8,128)(2,1)S(1)} fusion(bf16[32,640]{1,0:T(8,128)(2,1)S(1)} %bitcast.84, bf16[512,640]{1,0:T(8,128)(2,1)S(1)} %bitcast.70, bf16[640,608]{0,1:T(8,128)(2,1)} %param.12, bf16[640,608]{0,1:T(8,128)(2,1)} %param.11), kind=kOutput, calls=%fused_computation.9 | convolution fusion | flops 899932160 | bytes 3645440 | tf_op jit(solution)/shard_map/dot_general | solution.py:23
  41.6 2.7 %convolution_convert_fusion = bf16[544,1280]{1,0:T(8,128)(2,1)S(1)} fusion(bf16[640,1280]{0,1:T(8,128)(2,1)} %collective-permute-done, bf16[32,640]{1,0:T(8,128)(2,1)S(1)} %bitcast.85, bf16[512,640]{1,0:T(8,128)(2,1)S(1)} %bitcast.71), kind=kOutput, calls=%fused_computation.8 | convolution fusion | flops 893378560 | bytes 3727360 | tf_op jit(solution)/shard_map/dot_general | solution.py:23
  44.3 1.7 pad_maximum_fusion
  46.0 7.8 %all-to-all-start.1 = ((bf16[32,88,128]{2,1,0:T(8,128)(2,1)}), bf16[32,88,128]{2,1,0:T(8,128)(2,1)S(1)}, u32[]{:S(2)}, u32[]{:S(2)}) async-start(bf16[32,88,128]{2,1,0:T(8,128)(2,1)} %maximum_maximum_fusion.1), calls=%async_computation.2 | async-start | bytes 1441792 | tf_op jit(solution)/shard_map/all_to_all | solution.py:73
  53.9 2.2 pad_bitcast_fusion
  56.1 3.3 %collective-permute-start.4 = (bf16[640,640]{1,0:T(8,128)(2,1)}, bf16[640,640]{1,0:T(8,128)(2,1)}, u32[]{:S(2)}, u32[]{:S(2)}) collective-permute-start(bf16[640,640]{1,0:T(8,128)(2,1)} %get-tuple-element.49), channel_id=1, source_target_pairs={{0,8},{8,0},{16,24},{24,16},{32,40},{40,32},{48,56},{56,48},{64,72... | collective-permute-start | bytes 2457608 | tf_op jit(solution)/shard_map/ppermute | solution.py:78
  59.5 12.3 %all-to-all-done.1 = bf16[32,88,128]{2,1,0:T(8,128)(2,1)S(1)} async-done(((bf16[32,88,128]{2,1,0:T(8,128)(2,1)}), bf16[32,88,128]{2,1,0:T(8,128)(2,1)S(1)}, u32[]{:S(2)}, u32[]{:S(2)}) %all-to-all-start.1) | async-done | bytes 720928 | tf_op jit(solution)/shard_map/all_to_all | solution.py:73
  71.9 2.6 %fusion.7 = bf16[2,544,640]{2,1,0:T(8,128)(2,1)S(1)} fusion(bf16[1,640,640]{2,1,0:T(8,128)(2,1)} %bitcast.23, bf16[1,640,640]{2,1,0:T(8,128)(2,1)S(1)} %get-tuple-element.48, bf16[544,640]{1,0:T(8,128)(2,1)S(1)} %pad_maximum_fusion.4), kind=kOutput, calls=%fused_computation.17 | convolution fusion | flops 892805120 | bytes 3727360 | tf_op jit(solution)/shard_map/dot_general | solution.py:119
  74.5 47.9 %all_to_all.20 = bf16[8,136,640]{2,1,0:T(8,128)(2,1)S(1)} all-to-all(bf16[8,136,640]{2,1,0:T(8,128)(2,1)S(1)} %bitcast.76), channel_id=1, replica_groups=mesh['expert'=64,'tensor'=8] {'tensor'}, dimensions={0} | all-to-all | bytes 2785280 | tf_op jit(solution)/shard_map/all_to_all | solution.py:126
  122.7 1.2 fusion.31
  124.9 24.6 %all_gather.6 = bf16[1088,480]{1,0:T(8,128)(2,1)S(1)} all-gather(bf16[136,480]{1,0:T(8,128)(2,1)S(1)} %slice.104), channel_id=1, replica_groups=mesh['expert'=64,'tensor'=8] {'tensor'}, dimensions={0}, use_global_device_ids=true | all-gather | bytes 1175040 | tf_op jit(solution)/shard_map/all_gather | solution.py:137
  149.5 10.2 %collective-permute-start.2 = (bf16[544,640]{1,0:T(8,128)(2,1)S(1)}, bf16[544,640]{1,0:T(8,128)(2,1)S(1)}, u32[]{:S(2)}, u32[]{:S(2)}) collective-permute-start(bf16[544,640]{1,0:T(8,128)(2,1)S(1)} %pad_maximum_fusion.4), channel_id=1, source_target_pairs={{0,8},{8,0},{16,24},{24,16},{32,40},{40,32},{48,56},{56,48},{64,72... | collective-permute-start | bytes 2088968 | tf_op jit(solution)/shard_map/ppermute | solution.py:78
  159.8 1.9 collective-permute-start.1
  161.8 2.4 %collective-permute-start.3 = (bf16[544,640]{1,0:T(8,128)(2,1)S(1)}, bf16[544,640]{1,0:T(8,128)(2,1)S(1)}, u32[]{:S(2)}, u32[]{:S(2)}) collective-permute-start(bf16[544,640]{1,0:T(8,128)(2,1)S(1)} %pad_maximum_fusion.3), channel_id=1, source_target_pairs={{0,8},{8,0},{16,24},{24,16},{32,40},{40,32},{48,56},{56,48},{64,72... | collective-permute-start | bytes 2088968 | tf_op jit(solution)/shard_map/ppermute | solution.py:78
  164.4 1.1 convolution_convert_fusion.6
  165.9 1.2 pad_maximum_fusion.1
  167.1 10.1 %all-gather.2.cloned.1.call-done = bf16[1088,1408]{1,0:T(8,128)(2,1)} async-done(((bf16[136,1408]{1,0:T(8,128)(2,1)}), bf16[1088,1408]{1,0:T(8,128)(2,1)}) %all-gather.2.cloned.1.call-update) | async-done | bytes 3063824 | tf_op jit(solution)/shard_map/all_gather | solution.py:137
  177.3 3.2 %fusion.14 = f32[544,640]{1,0:T(8,128)S(1)} fusion(bf16[640,1280]{0,1:T(8,128)(2,1)} %collective-permute-done, bf16[1088,1408]{1,0:T(8,128)(2,1)} %all-gather.2.cloned.1.call-done), kind=kOutput, calls=%fused_computation.24 | convolution fusion | flops 891289600 | bytes 4423680 | tf_op jit(solution)/shard_map/dot_general | solution.py:23
  180.6 1.3 add_convert_fusion
  182.0 1.1 maximum_maximum_fusion.2
  183.1 2.4 %collective-permute-start.5 = (bf16[1088,1408]{1,0:T(8,128)(2,1)}, bf16[1088,1408]{1,0:T(8,128)(2,1)}, u32[]{:S(2)}, u32[]{:S(2)}) collective-permute-start(bf16[1088,1408]{1,0:T(8,128)(2,1)} %all-gather.2.cloned.1.call-done), channel_id=1, source_target_pairs={{0,8},{8,0},{16,24},{24,16},{32,40},{40,32},{48,56},{56,48},{64,72... | collective-permute-start | bytes 9191432 | tf_op jit(solution)/shard_map/ppermute | solution.py:78
  185.5 10.2 %all-to-all-start.3 = ((bf16[32,88,128]{2,1,0:T(8,128)(2,1)}), bf16[32,88,128]{2,1,0:T(8,128)(2,1)S(1)}, u32[]{:S(2)}, u32[]{:S(2)}) async-start(bf16[32,88,128]{2,1,0:T(8,128)(2,1)} %maximum_maximum_fusion.2), calls=%async_computation.4 | async-start | bytes 1441792 | tf_op jit(solution)/shard_map/all_to_all | solution.py:73
  195.7 1.5 slice.93
  197.2 1.5 slice.110
  200.9 2.3 %convolution_convert_fusion.2 = bf16[640,608]{0,1:T(8,128)(2,1)} fusion(bf16[1088,640]{1,0:T(8,128)(2,1)S(1)} %copy-done.1, bf16[544,1408]{1,0:T(8,128)(2,1)S(1)} %slice.93, bf16[544,1408]{1,0:T(8,128)(2,1)S(1)} %slice.110), kind=kOutput, calls=%fused_computation.18 | convolution fusion | flops 849760256 | bytes 5234688 | tf_op jit(solution)/shard_map/dot_general | solution.py:23
  203.2 2.3 %convolution_convert_fusion.3 = bf16[640,608]{0,1:T(8,128)(2,1)} fusion(bf16[1088,640]{1,0:T(8,128)(2,1)S(1)} %copy-done.1, bf16[544,1408]{1,0:T(8,128)(2,1)S(1)} %slice.93, bf16[544,1408]{1,0:T(8,128)(2,1)S(1)} %slice.110), kind=kOutput, calls=%fused_computation.19 | convolution fusion | flops 849760256 | bytes 5234688 | tf_op jit(solution)/shard_map/dot_general | solution.py:23
  205.5 8.9 %all-to-all-done.3 = bf16[32,88,128]{2,1,0:T(8,128)(2,1)S(1)} async-done(((bf16[32,88,128]{2,1,0:T(8,128)(2,1)}), bf16[32,88,128]{2,1,0:T(8,128)(2,1)S(1)}, u32[]{:S(2)}, u32[]{:S(2)}) %all-to-all-start.3) | async-done | bytes 720928 | tf_op jit(solution)/shard_map/all_to_all | solution.py:73
  (75 shorter events, 8.9 us)
Async XLA Ops:
  7.2 1.1 copy-start
  8.2 1.7 copy-start.5
  9.9 28.9 %all-to-all-start = ((bf16[32,88,128]{2,1,0:T(8,128)(2,1)}), bf16[32,88,128]{2,1,0:T(8,128)(2,1)S(1)}, u32[]{:S(2)}, u32[]{:S(2)}) async-start(bf16[32,88,128]{2,1,0:T(8,128)(2,1)} %maximum_maximum_fusion), calls=%async_computation | async-start | bytes 1441792 | tf_op jit(solution)/shard_map/all_to_all | solution.py:73
  20.5 4.5 %copy-start.8 = (f32[128,2]{0,1:T(2,128)S(1)}, f32[128,2]{0,1:T(2,128)}, u32[]{:S(2)}) copy-start(f32[128,2]{0,1:T(2,128)} %param.10) | copy-start | bytes 3076
  20.5 4.5 %copy-start.7 = (bf16[128,640]{1,0:T(8,128)(2,1)S(1)}, bf16[128,640]{1,0:T(8,128)(2,1)}, u32[]{:S(2)}) copy-start(bf16[128,640]{1,0:T(8,128)(2,1)} %param.8) | copy-start | bytes 491524
  20.5 102.2 %reduce-scatter.2.cloned.1.call-start = ((), (), s32[]{:S(2)}) async-start(), calls=%async_computation.5 | async-start | bytes 3133440 | tf_op jit(solution)/shard_map/reduce_scatter | solution.py:114
  22.1 19.5 %collective-permute-start = (bf16[640,1280]{0,1:T(8,128)(2,1)S(1)}, bf16[640,1280]{0,1:T(8,128)(2,1)}, u32[]{:S(2)}, u32[]{:S(2)}) collective-permute-start(bf16[640,1280]{0,1:T(8,128)(2,1)S(1)} %fusion.2), channel_id=1, source_target_pairs={{0,8},{8,0},{16,24},{24,16},{32,40},{40,32},{48,56},{56,48},{64,72... | collective-permute-start | bytes 4915208 | tf_op jit(solution)/shard_map/ppermute | solution.py:78
  46.0 25.7 %all-to-all-start.1 = ((bf16[32,88,128]{2,1,0:T(8,128)(2,1)}), bf16[32,88,128]{2,1,0:T(8,128)(2,1)S(1)}, u32[]{:S(2)}, u32[]{:S(2)}) async-start(bf16[32,88,128]{2,1,0:T(8,128)(2,1)} %maximum_maximum_fusion.1), calls=%async_computation.2 | async-start | bytes 1441792 | tf_op jit(solution)/shard_map/all_to_all | solution.py:73
  53.9 123.4 %all-gather.2.cloned.1.call-start = ((), (), s32[]{:S(2)}) async-start(), calls=%async_computation.6 | async-start | bytes 3446784 | tf_op jit(solution)/shard_map/all_gather | solution.py:137
  56.1 15.8 %collective-permute-start.4 = (bf16[640,640]{1,0:T(8,128)(2,1)}, bf16[640,640]{1,0:T(8,128)(2,1)}, u32[]{:S(2)}, u32[]{:S(2)}) collective-permute-start(bf16[640,640]{1,0:T(8,128)(2,1)} %get-tuple-element.49), channel_id=1, source_target_pairs={{0,8},{8,0},{16,24},{24,16},{32,40},{40,32},{48,56},{56,48},{64,72... | collective-permute-start | bytes 2457608 | tf_op jit(solution)/shard_map/ppermute | solution.py:78
  149.5 14.7 %collective-permute-start.2 = (bf16[544,640]{1,0:T(8,128)(2,1)S(1)}, bf16[544,640]{1,0:T(8,128)(2,1)S(1)}, u32[]{:S(2)}, u32[]{:S(2)}) collective-permute-start(bf16[544,640]{1,0:T(8,128)(2,1)S(1)} %pad_maximum_fusion.4), channel_id=1, source_target_pairs={{0,8},{8,0},{16,24},{24,16},{32,40},{40,32},{48,56},{56,48},{64,72... | collective-permute-start | bytes 2088968 | tf_op jit(solution)/shard_map/ppermute | solution.py:78
  159.8 4.5 %collective-permute-start.1 = (bf16[544,480]{1,0:T(8,128)(2,1)S(1)}, bf16[544,480]{1,0:T(8,128)(2,1)S(1)}, u32[]{:S(2)}, u32[]{:S(2)}) collective-permute-start(bf16[544,480]{1,0:T(8,128)(2,1)S(1)} %get-tuple-element.47), channel_id=1, source_target_pairs={{0,8},{8,0},{16,24},{24,16},{32,40},{40,32},{48,56},{56,48},{64,72... | collective-permute-start | bytes 1566728 | tf_op jit(solution)/shard_map/ppermute | solution.py:78
  161.8 4.2 %collective-permute-start.3 = (bf16[544,640]{1,0:T(8,128)(2,1)S(1)}, bf16[544,640]{1,0:T(8,128)(2,1)S(1)}, u32[]{:S(2)}, u32[]{:S(2)}) collective-permute-start(bf16[544,640]{1,0:T(8,128)(2,1)S(1)} %pad_maximum_fusion.3), channel_id=1, source_target_pairs={{0,8},{8,0},{16,24},{24,16},{32,40},{40,32},{48,56},{56,48},{64,72... | collective-permute-start | bytes 2088968 | tf_op jit(solution)/shard_map/ppermute | solution.py:78
  167.1 13.4 %copy-start.2 = (bf16[640,608]{0,1:T(8,128)(2,1)S(1)}, bf16[640,608]{0,1:T(8,128)(2,1)}, u32[]{:S(2)}) copy-start(bf16[640,608]{0,1:T(8,128)(2,1)} %param.12) | copy-start | bytes 2334724
  177.3 3.3 %copy-start.3 = (bf16[640,608]{0,1:T(8,128)(2,1)S(1)}, bf16[640,608]{0,1:T(8,128)(2,1)}, u32[]{:S(2)}) copy-start(bf16[640,608]{0,1:T(8,128)(2,1)} %param.11) | copy-start | bytes 2334724
  177.3 3.3 %copy-start.4 = (bf16[1088,1408]{1,0:T(8,128)(2,1)S(1)}, bf16[1088,1408]{1,0:T(8,128)(2,1)}, u32[]{:S(2)}) copy-start(bf16[1088,1408]{1,0:T(8,128)(2,1)} %all-gather.2.cloned.1.call-done) | copy-start | bytes 9191428
  183.1 14.1 %collective-permute-start.5 = (bf16[1088,1408]{1,0:T(8,128)(2,1)}, bf16[1088,1408]{1,0:T(8,128)(2,1)}, u32[]{:S(2)}, u32[]{:S(2)}) collective-permute-start(bf16[1088,1408]{1,0:T(8,128)(2,1)} %all-gather.2.cloned.1.call-done), channel_id=1, source_target_pairs={{0,8},{8,0},{16,24},{24,16},{32,40},{40,32},{48,56},{56,48},{64,72... | collective-permute-start | bytes 9191432 | tf_op jit(solution)/shard_map/ppermute | solution.py:78
  185.5 28.8 %all-to-all-start.3 = ((bf16[32,88,128]{2,1,0:T(8,128)(2,1)}), bf16[32,88,128]{2,1,0:T(8,128)(2,1)S(1)}, u32[]{:S(2)}, u32[]{:S(2)}) async-start(bf16[32,88,128]{2,1,0:T(8,128)(2,1)} %maximum_maximum_fusion.2), calls=%async_computation.4 | async-start | bytes 1441792 | tf_op jit(solution)/shard_map/all_to_all | solution.py:73
  199.2 1.6 copy-start.1
  205.5 9.0 %copy-start.6 = (pred[16,2,16,128]{3,2,1,0:T(8,128)(4,1)S(1)}, pred[16,2,16,128]{3,2,1,0:T(8,128)(4,1)}, u32[]{:S(2)}) copy-start(pred[16,2,16,128]{3,2,1,0:T(8,128)(4,1)} %copy-done.5) | copy-start | bytes 196612
Sparse Core Ops, SparseCore 0:
  46.2 56.9 reduce-scatter.1
  124.9 52.3 all-gather.1
